TPU v7x, 256 devices: a whole 4x4x8 slice. The times are simulated.
256 devices in a mesh: clus: 16 (over z, core), node: 16 (over x, y).
Axes of the slice: x: 4, y: 4, z: 8, core: 2. Of those that a mesh axis runs over, the one named last changes fastest.
Arguments:
- node_feats: bfloat16 [16, 2048, 1024], P('clus', 'node'), may hold values from -6 to 6
- cotangent: bfloat16 [16, 2048, 1024], P('clus', 'node'), may hold values from -6 to 6
- w_query: bfloat16 [1024, 1024], replicated, may hold values from -0.1875 to 0.1875
- w_key: bfloat16 [1024, 1024], replicated, may hold values from -0.1875 to 0.1875
- w_value: bfloat16 [1024, 1024], replicated, may hold values from -0.1875 to 0.1875
- w_out: bfloat16 [1024, 1024], replicated, may hold values from -0.1875 to 0.1875
- eigvec: bfloat16 [16, 64, 2048], P('clus'), may hold values from -3.5 to 3.5
- eig_weight: float32 [16, 64], P('node'), may hold values from 0.1 to 1
- block_mask: int32 [16, 16, 16, 16], P('clus', 'node'), may hold values from 0 to 1, as said below
Outputs:
- grad_nodes: bfloat16 [16, 2048, 1024], P('clus', 'node')
- grad_eigvec: float32 [16, 64, 2048], P('clus', None, 'node')
- grad_weight: float32 [16, 64], P('node')
- grad_proj: float32 [4, 1024, 1024], P(None, 'clus', 'node')
Inputs may be any that keep to these rules, and one draw needn't show every extreme that they name: `block_mask`: each entry is 0 or 1; every diagonal tile is 1; the share of present tiles differs between clusters and heads.
All inputs are finite; a program needn't handle non-finite values.
Results may differ from a plain program's by a relative error of at most 0.012.
The roundings to bfloat16 on the way count: a program that leaves them out, or rounds other values in their place, can miss the bound.
Values may be sent and summed in bfloat16 or wider, within the bound.
A program may use at most 128 MiB of HBM per device.

v0:
```python
import jax
import jax.numpy as jnp
from jax import lax
from jax.sharding import PartitionSpec as P


def body(node_feats, cotangent, w_query, w_key, w_value, w_out, eigvec, eig_weight, block_mask):
    node_rows = node_feats[0]
    grads_in = cotangent[0]
    query = jnp.dot(node_rows, w_query, preferred_element_type=jnp.float32).astype(jnp.bfloat16)
    keys_local = jnp.dot(node_rows, w_key, preferred_element_type=jnp.float32).astype(jnp.bfloat16)
    values_local = jnp.dot(node_rows, w_value, preferred_element_type=jnp.float32).astype(
        jnp.bfloat16
    )
    d_att = jnp.dot(grads_in, w_out, preferred_element_type=jnp.float32).astype(jnp.bfloat16)
    head_data = lax.all_to_all(
        jnp.stack([query, keys_local, values_local, d_att]),
        "node",
        split_axis=2,
        concat_axis=1,
        tiled=True,
    )
    node_count = head_data.shape[1]
    head_width = head_data.shape[2]
    heads_dev = eig_weight.shape[0]
    head_size = head_width // heads_dev
    by_head = head_data.reshape(4, node_count, heads_dev, head_size)
    query_heads = by_head[0]
    keys_heads = by_head[1]
    values_heads = by_head[2]
    dout_heads = by_head[3]
    eig_all = eigvec[0]
    eig_float = eig_all.astype(jnp.float32)
    weighted = (eig_weight[:, :, None] * eig_float[None]).astype(jnp.bfloat16)
    tile_mask = block_mask[0]
    tile_count = tile_mask.shape[2]
    tile_size = node_count // tile_count
    block_rows = min(512, node_count)
    block_count = node_count // block_rows
    score_scale = head_size ** (-0.5)

    def one_block(totals, block_index):
        key_grad, value_grad, eig_right, weight_grad = totals
        offset = block_index * block_rows
        query_block = lax.dynamic_slice_in_dim(query_heads, offset, block_rows, 0)
        dout_block = lax.dynamic_slice_in_dim(dout_heads, offset, block_rows, 0)
        eig_block = lax.dynamic_slice_in_dim(eig_all, offset, block_rows, 1)
        eig_bias = jnp.einsum(
            "ki,hkj->hij", eig_block, weighted, preferred_element_type=jnp.float32
        )
        scores = (
            jnp.einsum("ihd,jhd->hij", query_block, keys_heads, preferred_element_type=jnp.float32)
            * score_scale
            + eig_bias
        )
        tile_rows = lax.dynamic_slice_in_dim(
            tile_mask, offset // tile_size, block_rows // tile_size, 1
        )
        present = jnp.broadcast_to(
            tile_rows[:, :, None, :, None] > 0,
            (heads_dev, block_rows // tile_size, tile_size, tile_count, tile_size),
        )
        present = present.reshape(heads_dev, block_rows, node_count)
        masked = jnp.where(present, scores, -jnp.inf)
        row_max = jnp.max(masked, axis=2, keepdims=True)
        raised = jnp.exp(masked - row_max)
        attn_prob = raised / jnp.sum(raised, axis=2, keepdims=True)
        prob_half = attn_prob.astype(jnp.bfloat16)
        out_block = jnp.einsum(
            "hij,jhd->ihd", prob_half, values_heads, preferred_element_type=jnp.float32
        ).astype(jnp.bfloat16)
        dprob = jnp.einsum(
            "ihd,jhd->hij", dout_block, values_heads, preferred_element_type=jnp.float32
        )
        row_delta = jnp.sum(attn_prob * dprob, axis=2, keepdims=True)
        dscore = (attn_prob * (dprob - row_delta)).astype(jnp.bfloat16)
        query_grad = (
            jnp.einsum("hij,jhd->ihd", dscore, keys_heads, preferred_element_type=jnp.float32)
            * score_scale
        ).astype(jnp.bfloat16)
        key_grad = key_grad + jnp.einsum(
            "hij,ihd->jhd", dscore, query_block, preferred_element_type=jnp.float32
        )
        value_grad = value_grad + jnp.einsum(
            "hij,ihd->jhd", prob_half, dout_block, preferred_element_type=jnp.float32
        )
        eig_left = jnp.einsum("hij,kj->hki", dscore, eig_all, preferred_element_type=jnp.float32)
        weight_grad = weight_grad + jnp.sum(eig_left * eig_block.astype(jnp.float32)[None], axis=2)
        eig_right = eig_right + jnp.einsum(
            "hij,ki->hkj", dscore, eig_block, preferred_element_type=jnp.float32
        )
        left_term = jnp.sum(eig_weight[:, :, None] * eig_left, axis=0)
        return ((key_grad, value_grad, eig_right, weight_grad), (out_block, query_grad, left_term))

    initial = (
        jnp.zeros((node_count, heads_dev, head_size), jnp.float32),
        jnp.zeros((node_count, heads_dev, head_size), jnp.float32),
        jnp.zeros((heads_dev, eig_all.shape[0], node_count), jnp.float32),
        jnp.zeros(eig_weight.shape, jnp.float32),
    )
    totals, blocks = lax.scan(one_block, initial, jnp.arange(block_count))
    output_heads = blocks[0].reshape(node_count, head_width)
    query_grad_heads = blocks[1].reshape(node_count, head_width)
    key_grad_heads = (totals[0] * score_scale).astype(jnp.bfloat16).reshape(node_count, head_width)
    value_grad_heads = totals[1].astype(jnp.bfloat16).reshape(node_count, head_width)
    left_all = blocks[2].transpose(1, 0, 2).reshape(eig_all.shape[0], node_count)
    eig_term = left_all + jnp.sum(eig_weight[:, :, None] * totals[2], axis=0)
    returned = lax.all_to_all(
        jnp.stack([output_heads, query_grad_heads, key_grad_heads, value_grad_heads]),
        "node",
        split_axis=1,
        concat_axis=2,
        tiled=True,
    )
    output_nodes = returned[0]
    query_grad_nodes = returned[1]
    key_grad_nodes = returned[2]
    value_grad_nodes = returned[3]
    grad_rows = (
        jnp.einsum("re,de->rd", query_grad_nodes, w_query, preferred_element_type=jnp.float32)
        + jnp.einsum("re,de->rd", key_grad_nodes, w_key, preferred_element_type=jnp.float32)
        + jnp.einsum("re,de->rd", value_grad_nodes, w_value, preferred_element_type=jnp.float32)
    ).astype(jnp.bfloat16)
    grad_eigvec = lax.psum_scatter(eig_term, "node", scatter_dimension=1, tiled=True)
    grad_weight = lax.psum(totals[3], "clus")
    grad_terms = jnp.stack(
        [
            jnp.einsum(
                "rd,re->de", node_rows, query_grad_nodes, preferred_element_type=jnp.float32
            ),
            jnp.einsum("rd,re->de", node_rows, key_grad_nodes, preferred_element_type=jnp.float32),
            jnp.einsum(
                "rd,re->de", node_rows, value_grad_nodes, preferred_element_type=jnp.float32
            ),
            jnp.einsum("rd,re->de", grads_in, output_nodes, preferred_element_type=jnp.float32),
        ]
    )
    col_sums = lax.psum_scatter(grad_terms, "node", scatter_dimension=2, tiled=True)
    grad_proj = lax.psum_scatter(col_sums, "clus", scatter_dimension=1, tiled=True)
    return (grad_rows[None], grad_eigvec[None], grad_weight, grad_proj)


def solution(mesh):
    placed = (
        P("clus", "node", None),
        P("clus", "node", None),
        P(),
        P(),
        P(),
        P(),
        P("clus", None, None),
        P("node", None),
        P("clus", "node", None, None),
    )
    return jax.shard_map(
        body,
        mesh=mesh,
        in_specs=placed,
        out_specs=(
            P("clus", "node", None),
            P("clus", None, "node"),
            P("node", None),
            P(None, "clus", "node"),
        ),
        check_vma=False,
    )
```

profile of v0, /device:TPU:6, one launch (start us, length us, event | category | flops | bytes accessed | tf_op | source)
XLA Modules:
  0.0 431.3 jit_solution(2810686122069880913)
XLA Ops:
  7.2 1.5 copy-done
  8.8 1.8 fusion.53
  10.6 2.1 fusion.54
  13.8 1.4 copy.40
  15.3 7.4 %all-to-all-start = ((bf16[4,128,1024]{1,0,2:T(4,128)(2,1)}), bf16[4,128,1024]{1,0,2:T(4,128)(2,1)S(1)}, u32[]{:S(2)}, u32[]{:S(2)}) async-start(bf16[4,128,1024]{1,0,2:T(4,128)(2,1)} %copy.40), calls=%async_computation | async-start | bytes 2097152 | tf_op jit(solution)/shard_map/all_to_all | solution.py:16
  23.7 14.3 %all-to-all-done = bf16[4,128,1024]{1,0,2:T(4,128)(2,1)S(1)} async-done(((bf16[4,128,1024]{1,0,2:T(4,128)(2,1)}), bf16[4,128,1024]{1,0,2:T(4,128)(2,1)S(1)}, u32[]{:S(2)}, u32[]{:S(2)}) %all-to-all-start) | async-done | bytes 1048608 | tf_op jit(solution)/shard_map/all_to_all | solution.py:16
  41.5 74.0 %while.25 = (s32[]{:T(128)}, f32[2048,1,64]{0,2,1:T(8,128)}, f32[2048,1,64]{0,2,1:T(8,128)}, f32[1,64,2048]{2,1,0:T(8,128)}, f32[1,64]{1,0:T(1,128)S(1)}, /*inde...) while((s32[]{:T(128)}, f32[2048,1,64]{0,2,1:T(8,128)}, ...), condition=%wide.region_5.6_spmd.clone, body=%wide.region_0.5_spmd.clone.sunk | while | flops 1224702592 | bytes 83313016 | solution.py:101
  43.8 2.3 broadcast_in_dim.70
  46.1 1.7 fusion.131
  47.8 1.3 fusion.132
  50.1 1.3 fusion.134
  51.8 0.9 multiply_reduce_fusion.2
  52.7 1.4 fusion.141
  54.1 1.4 fusion.140
  57.4 2.3 fusion.136
  62.0 2.3 broadcast_in_dim.70
  64.3 1.7 fusion.131
  66.0 1.3 fusion.132
  68.3 1.3 fusion.134
  70.0 0.9 multiply_reduce_fusion.2
  70.9 1.4 fusion.141
  72.3 1.4 fusion.140
  74.3 0.9 bitcast_dynamic-update-slice_fusion.2
  75.7 2.6 fusion.136
  80.7 2.3 broadcast_in_dim.70
  82.9 1.7 fusion.131
  84.7 1.3 fusion.132
  87.0 1.3 fusion.134
  88.7 0.9 multiply_reduce_fusion.2
  89.5 1.4 fusion.141
  90.9 1.4 fusion.140
  92.9 0.9 bitcast_dynamic-update-slice_fusion.2
  94.3 2.6 fusion.136
  99.2 2.3 broadcast_in_dim.70
  101.5 1.7 fusion.131
  103.3 1.3 fusion.132
  105.6 1.3 fusion.134
  107.3 0.9 multiply_reduce_fusion.2
  108.1 1.4 fusion.141
  109.5 1.4 fusion.140
  111.5 0.8 bitcast_dynamic-update-slice_fusion.2
  112.9 2.6 fusion.136
  115.5 1.2 copy.46
  116.9 1.2 copy.47
  118.0 0.9 stack_reshape.13
  118.9 1.3 fusion.57
  120.2 1.1 pad_maximum_fusion.2
  121.3 2.5 copy.48
  123.8 4.4 %reshape.203 = bf16[16,2,16384]{2,1,0:T(2,128)(2,1)S(1)} reshape(bf16[2048,4,64]{2,1,0:T(4,128)(2,1)} %bitcast.283) | data formatting | bytes 2097152
  128.1 19.2 %all_to_all.30 = bf16[16,2,16384]{2,1,0:T(2,128)(2,1)} all-to-all(bf16[16,2,16384]{2,1,0:T(2,128)(2,1)S(1)} %reshape.203), channel_id=1, replica_groups=mesh['clus'=16,'node'=16] {'node'}, dimensions={0} | all-to-all | bytes 2097152 | tf_op jit(solution)/shard_map/all_to_all | solution.py:108
  147.4 5.2 %reshape.204 = bf16[2048,4,64]{2,1,0:T(4,128)(2,1)} reshape(bf16[16,2,16384]{2,1,0:T(2,128)(2,1)} %all_to_all.30) | data formatting | bytes 2097152
  152.6 2.8 copy.56
  158.7 6.0 %pad_maximum_fusion = f32[4,1024,1024]{1,2,0:T(8,128)} fusion(f32[1,1024,1024]{1,2,0:T(8,128)S(1)} %convolution_bitcast_fusion.4, f32[1,1024,1024]{1,2,0:T(8,128)S(1)} %convolution_bitcast_fusion.5, f32[1,1024,1024]{1,2,0:T(8,128)S(1)} %convolution_bitcast_fusion.6, f32[1,1024,1024]{1,2,0:T(8,128)S(1)} %convolution_bitcast_fusion.7), kind=kLoop, calls=%fused_computation.58 | loop fusion | flops 12582912 | bytes 33554432 | tf_op jit(solution)/shard_map/stack | solution.py:126
  164.8 116.5 %reduce-scatter.8.cloned.1.call-done = f32[4,1024,64]{1,2,0:T(8,128)} async-done(((f32[4,1024,1024]{1,2,0:T(8,128)}), f32[4,1024,64]{1,2,0:T(8,128)}) %reduce-scatter.8.cloned.1.call-update) | async-done | bytes 1048592 | tf_op jit(solution)/shard_map/reduce_scatter | solution.py:138
  281.3 2.7 copy.57
  284.1 3.2 reshape.201
  287.4 1.1 copy.60
  288.5 0.9 bitcast_add_fusion.1
  289.4 26.9 %psum.7 = f32[1,64]{1,0:T(1,128)} all-reduce(f32[1,64]{1,0:T(1,128)S(1)} %get-tuple-element.549), channel_id=1, replica_groups=mesh['clus'=16,'node'=16] {'clus'}, use_global_device_ids=true, to_apply=%region_7.8 | all-reduce | flops 64 | bytes 512 | tf_op jit(solution)/shard_map/psum | solution.py:125
  317.1 2.4 convolution_add_fusion.1
  319.5 1.6 fusion.52
  321.1 23.5 %reduce-scatter.10.cloned.1.call-done = f32[64,256]{1,0:T(8,128)} async-done(((f32[1024,256]{1,0:T(8,128)}), f32[64,256]{1,0:T(8,128)}) %reduce-scatter.10.cloned.1.call-update) | async-done | bytes 65552
  344.6 0.9 reshape.202
  346.2 78.6 %reduce-scatter.6.cloned.1.call-done = f32[64,128]{1,0:T(8,128)} async-done(((f32[64,2048]{1,0:T(8,128)}), f32[64,128]{1,0:T(8,128)}) %reduce-scatter.6.cloned.1.call-update) | async-done | bytes 32784 | tf_op jit(solution)/shard_map/reduce_scatter | solution.py:124
  (166 shorter events, 28.2 us)
Async XLA Ops:
  7.2 1.6 copy-start
  7.2 5.6 %copy-start.9 = (bf16[1,128,1024]{2,1,0:T(8,128)(2,1)S(1)}, bf16[1,128,1024]{2,1,0:T(8,128)(2,1)}, u32[]{:S(2)}) copy-start(bf16[1,128,1024]{2,1,0:T(8,128)(2,1)} %param.11) | copy-start | bytes 786436
  7.2 5.5 %copy-start.13 = (bf16[1024,1024]{1,0:T(8,128)(2,1)S(1)}, bf16[1024,1024]{1,0:T(8,128)(2,1)}, u32[]{:S(2)}) copy-start(bf16[1024,1024]{1,0:T(8,128)(2,1)} %param.15) | copy-start | bytes 6291460
  7.2 6.0 %copy-start.17 = (bf16[1,128,1024]{2,1,0:T(8,128)(2,1)S(1)}, bf16[1,128,1024]{2,1,0:T(8,128)(2,1)}, u32[]{:S(2)}) copy-start(bf16[1,128,1024]{2,1,0:T(8,128)(2,1)} %param.12) | copy-start | bytes 786436
  7.2 6.0 %copy-start.15 = (bf16[1024,1024]{1,0:T(8,128)(2,1)S(1)}, bf16[1024,1024]{1,0:T(8,128)(2,1)}, u32[]{:S(2)}) copy-start(bf16[1024,1024]{1,0:T(8,128)(2,1)} %param.16) | copy-start | bytes 6291460
  13.2 9.6 %copy-start.2 = (bf16[1,64,2048]{2,1,0:T(8,128)(2,1)S(1)}, bf16[1,64,2048]{2,1,0:T(8,128)(2,1)}, u32[]{:S(2)}) copy-start(bf16[1,64,2048]{2,1,0:T(8,128)(2,1)} %param.17) | copy-start | bytes 786436
  13.2 9.6 %copy-start.19 = (f32[1,64]{1,0:T(1,128)S(1)}, f32[1,64]{1,0:T(1,128)}, u32[]{:S(2)}) copy-start(f32[1,64]{1,0:T(1,128)} %param.18) | copy-start | bytes 772
  15.3 22.7 %all-to-all-start = ((bf16[4,128,1024]{1,0,2:T(4,128)(2,1)}), bf16[4,128,1024]{1,0,2:T(4,128)(2,1)S(1)}, u32[]{:S(2)}, u32[]{:S(2)}) async-start(bf16[4,128,1024]{1,0,2:T(4,128)(2,1)} %copy.40), calls=%async_computation | async-start | bytes 2097152 | tf_op jit(solution)/shard_map/all_to_all | solution.py:16
  22.7 258.6 %reduce-scatter.8.cloned.1.call-start = ((), (), s32[]{:S(2)}) async-start(), calls=%async_computation.6 | async-start | bytes 17825792 | tf_op jit(solution)/shard_map/reduce_scatter | solution.py:138
  46.1 1.7 copy-start.1
  46.1 1.7 copy-start.3
  46.1 1.7 copy-start.11
  49.1 1.0 copy-start.12
  49.1 1.0 copy-start.16
  51.8 3.7 copy-start.4
  54.1 2.8 copy-start.6
  56.0 3.7 copy-start.5
  57.4 2.3 copy-start.7
  64.3 1.7 copy-start.1
  64.3 1.7 copy-start.3
  64.3 1.7 copy-start.11
  67.3 1.0 copy-start.12
  67.3 1.0 copy-start.16
  70.0 3.7 copy-start.4
  72.3 2.8 copy-start.6
  74.3 4.1 copy-start.5
  75.7 2.6 copy-start.7
  82.9 1.7 copy-start.1
  82.9 1.7 copy-start.3
  82.9 1.7 copy-start.11
  85.9 1.0 copy-start.12
  85.9 1.0 copy-start.16
  88.7 3.7 copy-start.4
  90.9 2.8 copy-start.6
  92.9 4.0 copy-start.5
  94.3 2.6 copy-start.7
  101.5 1.7 copy-start.1
  101.5 1.7 copy-start.3
  101.5 1.7 copy-start.11
  104.5 1.0 copy-start.12
  104.5 1.0 copy-start.16
  107.3 3.7 copy-start.4
  109.5 2.8 copy-start.6
  111.5 4.0 copy-start.5
  112.9 2.6 copy-start.7
  152.6 3.3 copy-start.10
  156.6 1.4 copy-start.18
  164.8 123.7 %copy-start.8 = (f32[1,64,2048]{2,1,0:T(8,128)S(1)}, f32[1,64,2048]{2,1,0:T(8,128)}, u32[]{:S(2)}) copy-start(f32[1,64,2048]{2,1,0:T(8,128)} %get-tuple-element.548) | copy-start | bytes 1572868
  164.8 179.9 %reduce-scatter.10.cloned.1.call-start = ((), (), s32[]{:S(2)}) async-start(), calls=%async_computation.7 | async-start | bytes 1114112
  287.3 137.5 %reduce-scatter.6.cloned.1.call-start = ((), (), s32[]{:S(2)}) async-start(), calls=%async_computation.5 | async-start | bytes 557056 | tf_op jit(solution)/shard_map/reduce_scatter | solution.py:124
  316.3 3.3 copy-start.14
Sparse Core Ops, SparseCore 0:
  164.9 116.4 reduce-scatter.7
  287.4 57.1 reduce-scatter.9
  349.1 75.6 reduce-scatter.5
where the time goes:
time: 433 us; the launch traced here: 431 us
  waiting for transfers between devices  233 us (54%)
  matrix products  58.3 us (13%)
  local copies, waits for them, and re-layouts  48.1 us (11%)
  blocking collectives  46.1 us (11%)
  other arithmetic  21.1 us (5%)
  between operations  14.2 us (3%)
  starting transfers between devices  7.55 us (2%)
    reduce_scatter x1, waiting for transfers between devices, body(): lax.psum_scatter(grad_terms, 'node', scatter_dimension=2, tiled=True)  117 us
    reduce_scatter x1, waiting for transfers between devices, body(): lax.psum_scatter(eig_term, 'node', scatter_dimension=1, tiled=True)  78.6 us
    psum x1, blocking collectives, body(): grad_weight = lax.psum(totals[3], 'clus')  26.9 us
    unnamed x4, waiting for transfers between devices  23.6 us
    all_to_all x1, blocking collectives, body(): lax.all_to_all(jnp.stack([output_heads, query_grad_heads, key_grad_heads,...  19.2 us
    unnamed x28, local copies, waits for them, and re-layouts  18.8 us
    all_to_all x1, waiting for transfers between devices, body(): lax.all_to_all(jnp.stack([query, keys_local, values_local, d_att]), 'node...  14.3 us
    broadcast_in_dim x8, local copies, waits for them, and re-layouts, one_block(): jnp.broadcast_to(tile_rows[:, :, None, :, None] > 0, (heads_dev, block_ro...  10.5 us
  transfers between devices with their start and end apart: 4, of which 4 were waited for; matrix products, arithmetic and copies ran while one was open for 2% of the time, Pallas kernels for 0%

commit v1 on v0

v1 whole, which is shorter than its diff:
```python
import functools

import jax
import jax.numpy as jnp
from jax import lax
from jax.experimental import pallas as pl
from jax.experimental.pallas import tpu as pltpu
from jax.sharding import PartitionSpec as P

MESH = pl.DeviceIdType.MESH
F32 = jnp.float32
BF16 = jnp.bfloat16
ABSENT = -(2.0**100)
SIDE = 4
NODES = 16
TOK = 128
D = 1024
NC = 2048
EIG = 64
HS = 64
SCALE = HS**-0.5
ROWS = 256


def dot(a, b):
    return lax.dot_general(a, b, (((1,), (0,)), ((), ())), preferred_element_type=F32)


def kernel(
    clusters,
    x_hbm, cot_hbm, wq_hbm, wk_hbm, wv_hbm, wo_hbm, eig_ref, lam_ref, mask_ref,
    gn_ref, ge_ref, gw_ref, gp_ref,
    w, xg, cg, send, recv, eigt, qe, d0, ke, bm, eqt, dt, kt, bt,
    acc_k, acc_v, grads, left, back, gs, gr,
    in_sem, w_sem, ring_send, ring_recv, f_send, f_recv, b_send, b_recv, c_send, c_recv,
):
    n = lax.axis_index("node")
    c = lax.axis_index("clus")
    mx = lax.div(n, SIDE)
    my = lax.rem(n, SIDE)
    chunk = D // clusters

    def turn(i, by):
        return lax.rem(i + by, SIDE)

    x_in = pltpu.make_async_copy(x_hbm, xg.at[mx, my], in_sem.at[0])
    c_in = pltpu.make_async_copy(cot_hbm, cg.at[mx, my], in_sem.at[1])
    x_in.start()
    c_in.start()
    w_hbm = (wq_hbm, wk_hbm, wv_hbm, wo_hbm)

    def w_copy(t, k):
        cols = pl.ds(pl.multiple_of(turn(mx, k) * 256, 256), 256)
        return pltpu.make_async_copy(w_hbm[t].at[:, cols], w.at[t, :, cols], w_sem.at[t, k])

    for k in range(SIDE):
        for t in range(4):
            w_copy(t, k).start()

    barrier = pltpu.get_barrier_semaphore()

    @pl.loop(1, NODES)
    def _(k):
        pl.semaphore_signal(barrier, inc=1, device_id={"node": lax.rem(n + k, NODES)}, device_id_type=MESH)

    if clusters > 1:
        @pl.loop(1, clusters)
        def _(k):
            pl.semaphore_signal(
                barrier, inc=1, device_id={"clus": lax.rem(c + k, clusters)}, device_id_type=MESH
            )

    row_id = lax.broadcasted_iota(jnp.int32, (EIG, EIG), 0)
    col_id = lax.broadcasted_iota(jnp.int32, (EIG, EIG), 1)
    lam = jnp.sum(jnp.where(row_id == col_id, lam_ref[...], 0.0), axis=1, keepdims=True)
    kt[64:128, :] = (lam * eig_ref[...].astype(F32)).astype(BF16)
    kt[144:256, :] = jnp.zeros((112, NC), BF16)
    bias = jnp.where(mask_ref[...] > 0, 0.0, ABSENT)
    for j in range(NODES):
        kt[128:144, j * TOK : (j + 1) * TOK] = jnp.broadcast_to(bias[:, j : j + 1], (16, TOK)).astype(BF16)
        part = eig_ref[:, j * TOK : (j + 1) * TOK].astype(F32)
        full = jnp.concatenate([jnp.zeros((64, TOK), F32), part], axis=0)
        eigt[j * TOK : (j + 1) * TOK, :] = full.T.astype(BF16)
    eqt[64:128, :] = eig_ref[...]

    x_in.wait()
    c_in.wait()
    pl.semaphore_wait(barrier, NODES - 1 + clusters - 1)

    def copy_to(src, dst, send_sem, recv_sem, node):
        return pltpu.make_async_remote_copy(
            src_ref=src, dst_ref=dst, send_sem=send_sem, recv_sem=recv_sem,
            device_id={"node": node}, device_id_type=MESH,
        )

    def x_line(i, lo, size):
        return xg.at[mx, i, pl.ds(lo, size)]

    def c_line(i, lo, size):
        return cg.at[i, my, pl.ds(lo, size)]

    def x_group(i, half):
        return xg.at[i, pl.ds(2 * half, 2)]

    def c_group(i, half):
        return cg.at[pl.ds(2 * half, 2), i]

    def x_along(by):
        return mx * SIDE + turn(my, by)

    def c_along(by):
        return turn(mx, by) * SIDE + my

    rings = []
    for which, line, group, one, two, p1, p2 in (
        (0, x_line, x_group, x_along, c_along, my, mx),
        (1, c_line, c_group, c_along, x_along, mx, my),
    ):
        rings.append((
            [(0, line(p1, 0, TOK), line(turn(p1, 3), 0, TOK), one(1)),
             (1, line(p1, 0, TOK), line(turn(p1, 1), 0, TOK), one(3))],
            [(2, line(turn(p1, 3), 0, 64), line(turn(p1, 2), 0, 64), one(1)),
             (3, line(turn(p1, 1), 64, 64), line(turn(p1, 2), 64, 64), one(3))],
            [(4, group(p2, 0), group(turn(p2, 3), 0), two(1)),
             (5, group(p2, 1), group(turn(p2, 1), 1), two(3))],
            [(6, group(p2, 1), group(turn(p2, 3), 1), two(1)),
             (7, group(p2, 0), group(turn(p2, 1), 0), two(3))],
            [(8, group(turn(p2, 3), 0), group(turn(p2, 2), 0), two(1)),
             (9, group(turn(p2, 1), 1), group(turn(p2, 2), 1), two(3))],
        ))

    def ring(stage, action):
        for which in range(2):
            for number, out, into, node in rings[which][stage]:
                sems = ring_send.at[which, number], ring_recv.at[which, number]
                if action == "start":
                    copy_to(out, out, *sems, node).start()
                elif action == "recv":
                    copy_to(into, into, *sems, node).wait_recv()
                else:
                    copy_to(out, out, *sems, node).wait_send()

    ring(0, "start")

    low = lax.broadcasted_iota(jnp.int32, (TOK, 128), 1) < 64

    def forward(t):
        return copy_to(send.at[t], recv.at[n], f_send.at[t], f_recv.at[n], t)

    def forward_self():
        return pltpu.make_async_copy(send.at[n], recv.at[n], f_recv.at[n])

    for k in range(SIDE):
        first = turn(mx, k) * SIDE
        cols = pl.ds(pl.multiple_of(first * HS, 256), 256)
        rows_x = xg[mx, my]
        parts = []
        for t in range(4):
            w_copy(t, k).wait()
            rows_in = rows_x if t < 3 else cg[mx, my]
            part = dot(rows_in, w[t, :, cols])
            parts.append(part * SCALE if t == 0 else part)
        for pair in range(2):
            q, kk, v, d = (part[:, pair * 128 : (pair + 1) * 128] for part in parts)
            qs, ks, vs, ds = (pltpu.roll(a, 64, 1) for a in (q, kk, v, d))
            t0 = first + 2 * pair
            send[t0, :, 0:128] = jnp.where(low, q, ds).astype(BF16)
            send[t0, :, 128:256] = jnp.where(low, kk, vs).astype(BF16)
            send[t0 + 1, :, 0:128] = jnp.where(low, qs, d).astype(BF16)
            send[t0 + 1, :, 128:256] = jnp.where(low, ks, v).astype(BF16)
        for j in range(SIDE):
            t = first + j

            @pl.when(t != n)
            def _():
                forward(t).start()

            @pl.when(t == n)
            def _():
                forward_self().start()

    ring(0, "recv")
    ring(1, "start")

    acc_k[...] = jnp.zeros_like(acc_k)
    acc_v[...] = jnp.zeros_like(acc_v)

    @pl.loop(0, NODES)
    def _(k):
        s = lax.rem(n + k, NODES)

        @pl.when(s != n)
        def _():
            copy_to(recv.at[s], recv.at[s], f_send.at[s], f_recv.at[s], s).wait_recv()

        @pl.when(s == n)
        def _():
            forward_self().wait()

        rows = pl.ds(pl.multiple_of(s * TOK, TOK), TOK)
        a = recv[s, :, 0:128].astype(F32)
        b = recv[s, :, 128:256].astype(F32)
        e = eigt[rows, :].astype(F32)
        qe[rows, :] = jnp.where(low, a, e).astype(BF16)
        ke[rows, :] = jnp.where(low, b, e).astype(BF16)
        d0[rows, :] = jnp.where(low, 0.0, a).astype(BF16)
        bm[rows, :] = b.astype(BF16)
        at = a.T.astype(BF16)
        b_t = b.T.astype(BF16)
        eqt[0:64, rows] = at[0:64]
        dt[:, rows] = at[64:128]
        kt[0:64, rows] = b_t[0:64]
        bt[:, rows] = b_t

    ring(1, "recv")
    ring(2, "start")
    ring(3, "start")

    lane = lax.broadcasted_iota(jnp.int32, (ROWS, 128), 1)
    sub = lax.div(lax.broadcasted_iota(jnp.int32, (ROWS, 128), 0), TOK)
    steps = NC // ROWS

    @pl.loop(0, steps)
    def _(i):
        @pl.when(i == steps // 2)
        def _():
            ring(2, "recv")
            ring(4, "start")

        rows = pl.ds(pl.multiple_of(i * ROWS, ROWS), ROWS)
        tile = jnp.where(lane == sub + i * (ROWS // TOK), 1.0, 0.0).astype(BF16)
        scores = dot(jnp.concatenate([qe[rows, :], tile], axis=1), kt[...])
        dprob = dot(d0[rows, :], bt[...])
        raised = jnp.exp(scores - jnp.max(scores, axis=1, keepdims=True))
        inverse = 1.0 / jnp.sum(raised, axis=1, keepdims=True)
        prob = raised * inverse
        delta = jnp.sum(prob * dprob, axis=1, keepdims=True)
        half = prob.astype(BF16)
        dscore = (prob * (dprob - delta)).astype(BF16)
        out = dot(half, bm[...])
        grad_q = dot(dscore, ke[...])
        acc_k[...] += dot(eqt[:, rows], dscore)
        acc_v[...] += dot(dt[:, rows], half)
        grad_qt = grad_q.T
        grads[0, :, rows] = (grad_qt[0:64] * SCALE).astype(BF16)
        left[:, rows] = grad_qt[64:128]
        grads[4, :, rows] = out.T[64:128].astype(BF16)

    grads[1] = acc_k[0:64].astype(BF16)
    grads[2] = acc_v[...].astype(BF16)
    left_all = left[...]
    grads[3] = (lam * (left_all + acc_k[64:128])).astype(BF16)

    def backward(t):
        return copy_to(
            grads.at[pl.ds(0, 4), :, pl.ds(pl.multiple_of(t * TOK, TOK), TOK)],
            back.at[:, pl.ds(pl.multiple_of(n * HS, HS), HS), :],
            b_send.at[t], b_recv.at[n], t,
        )

    def landed(s):
        return back.at[:, pl.ds(pl.multiple_of(s * HS, HS), HS), :]

    def backward_self():
        return pltpu.make_async_copy(
            grads.at[pl.ds(0, 4), :, pl.ds(pl.multiple_of(n * TOK, TOK), TOK)], landed(n), b_recv.at[n]
        )

    backward_self().start()

    @pl.loop(1, NODES)
    def _(k):
        backward(lax.rem(n + k, NODES)).start()

    weight_col = jnp.sum(eig_ref[...].astype(F32) * left_all, axis=1, keepdims=True)
    row_w = lax.broadcasted_iota(jnp.int32, (EIG, 256), 0)
    col_w = lax.broadcasted_iota(jnp.int32, (EIG, 256), 1)
    weight_row = jnp.sum(jnp.where(row_w == col_w, weight_col, 0.0), axis=0, keepdims=True)
    weight_high = weight_row.astype(BF16).astype(F32)
    row_g = lax.broadcasted_iota(jnp.int32, (16, 256), 0)
    weight_part = jnp.where(
        row_g == 0, weight_high, jnp.where(row_g == 1, weight_row - weight_high, 0.0)
    ).astype(BF16)

    ring(3, "recv")
    ring(4, "recv")

    def across(t):
        return pltpu.make_async_remote_copy(
            src_ref=gs.at[t], dst_ref=gr.at[c], send_sem=c_send.at[t], recv_sem=c_recv.at[c],
            device_id={"clus": t}, device_id_type=MESH,
        )

    def across_in(s):
        return pltpu.make_async_remote_copy(
            src_ref=gr.at[s], dst_ref=gr.at[s], send_sem=c_send.at[s], recv_sem=c_recv.at[s],
            device_id={"clus": s}, device_id_type=MESH,
        )

    def across_self():
        return pltpu.make_async_copy(gs.at[c], gr.at[c], c_recv.at[c])

    for m in range(4):
        cols = slice(m * 256, (m + 1) * 256)
        gx = dot(grads[0:3].reshape(192, NC), xg[:, :, :, cols].reshape(NC, 256))
        gc = dot(grads[4], cg[:, :, :, cols].reshape(NC, 256))
        g = jnp.concatenate([gx, gc], axis=0).T.astype(BF16)
        size = min(chunk, 256)
        for part in range(256 // size):
            owner, lo = divmod(m * 256 + part * size, chunk)
            gs[owner, lo : lo + size, :] = g[part * size : (part + 1) * size]
            if lo + size == chunk:
                gs[owner, chunk : chunk + 16, :] = weight_part

                @pl.when(c != owner)
                def _():
                    across(owner).start()

                @pl.when(c == owner)
                def _():
                    across_self().start()

    backward_self().wait()

    @pl.loop(1, NODES)
    def _(k):
        s = lax.rem(n + k, NODES)
        copy_to(landed(s), landed(s), b_send.at[s], b_recv.at[s], s).wait_recv()

    for m in range(4):
        rows = slice(m * 256, (m + 1) * 256)
        total = dot(w[0, rows, :], back[0]) + dot(w[1, rows, :], back[1]) + dot(w[2, rows, :], back[2])
        gn_ref[:, rows] = total.T.astype(BF16)
    eig_total = back[3, 0:64, :].astype(F32)
    for s in range(1, NODES):
        eig_total += back[3, s * 64 : (s + 1) * 64, :].astype(F32)
    ge_ref[...] = eig_total

    across_self().wait()
    if clusters > 1:
        @pl.loop(1, clusters)
        def _(k):
            across_in(lax.rem(c + k, clusters)).wait_recv()

    total = gr[0].astype(F32)
    for s in range(1, clusters):
        total += gr[s].astype(F32)
    for pair in range(2):
        both = total[0:chunk, pair * 128 : (pair + 1) * 128]
        gp_ref[2 * pair] = both[:, 0:64]
        gp_ref[2 * pair + 1] = pltpu.roll(both, 64, 1)[:, 0:64]
    gw_ref[...] = (total[chunk : chunk + 1] + total[chunk + 1 : chunk + 2])[:, 0:64]

    for stage in range(5):
        ring(stage, "send")

    @pl.loop(1, NODES)
    def _(k):
        t = lax.rem(n + k, NODES)
        forward(t).wait_send()
        backward(t).wait_send()

    if clusters > 1:
        @pl.loop(1, clusters)
        def _(k):
            across(lax.rem(c + k, clusters)).wait_send()


def body(clusters, node_feats, cotangent, w_query, w_key, w_value, w_out, eigvec, eig_weight, block_mask):
    chunk = D // clusters
    anywhere = pl.BlockSpec(memory_space=pl.ANY)
    vmem = pl.BlockSpec(memory_space=pltpu.VMEM)
    dma = pltpu.SemaphoreType.DMA
    gn, ge, gw, gp = pl.pallas_call(
        functools.partial(kernel, clusters),
        out_shape=(
            jax.ShapeDtypeStruct((TOK, D), BF16),
            jax.ShapeDtypeStruct((EIG, TOK), F32),
            jax.ShapeDtypeStruct((1, EIG), F32),
            jax.ShapeDtypeStruct((4, chunk, HS), F32),
        ),
        in_specs=[anywhere] * 6 + [vmem] * 3,
        out_specs=(vmem,) * 4,
        scratch_shapes=[
            pltpu.VMEM((4, D, D), BF16),
            pltpu.VMEM((SIDE, SIDE, TOK, D), BF16),
            pltpu.VMEM((SIDE, SIDE, TOK, D), BF16),
            pltpu.VMEM((NODES, TOK, 256), BF16),
            pltpu.VMEM((NODES, TOK, 256), BF16),
            pltpu.VMEM((NC, 128), BF16),
            pltpu.VMEM((NC, 128), BF16),
            pltpu.VMEM((NC, 128), BF16),
            pltpu.VMEM((NC, 128), BF16),
            pltpu.VMEM((NC, 128), BF16),
            pltpu.VMEM((128, NC), BF16),
            pltpu.VMEM((64, NC), BF16),
            pltpu.VMEM((256, NC), BF16),
            pltpu.VMEM((128, NC), BF16),
            pltpu.VMEM((128, NC), F32),
            pltpu.VMEM((64, NC), F32),
            pltpu.VMEM((5, 64, NC), BF16),
            pltpu.VMEM((64, NC), F32),
            pltpu.VMEM((4, D, TOK), BF16),
            pltpu.VMEM((clusters, chunk + 16, 256), BF16),
            pltpu.VMEM((clusters, chunk + 16, 256), BF16),
            dma((2,)),
            dma((4, 4)),
            dma((2, 10)),
            dma((2, 10)),
            dma((NODES,)),
            dma((NODES,)),
            dma((NODES,)),
            dma((NODES,)),
            dma((clusters,)),
            dma((clusters,)),
        ],
        compiler_params=pltpu.CompilerParams(
            collective_id=0, has_side_effects=True, vmem_limit_bytes=60 * 1024 * 1024
        ),
        cost_estimate=pl.CostEstimate(flops=8 * 10**9, bytes_accessed=10**7, transcendentals=4 * 10**6),
    )(
        node_feats[0], cotangent[0], w_query, w_key, w_value, w_out,
        eigvec[0], eig_weight, block_mask[0, 0],
    )
    return gn[None], ge[None], gw, gp


def solution(mesh):
    placed = (
        P("clus", "node", None),
        P("clus", "node", None),
        P(),
        P(),
        P(),
        P(),
        P("clus", None, None),
        P("node", None),
        P("clus", "node", None, None),
    )
    return jax.shard_map(
        functools.partial(body, mesh.shape["clus"]),
        mesh=mesh,
        in_specs=placed,
        out_specs=(
            P("clus", "node", None),
            P("clus", None, "node"),
            P("node", None),
            P(None, "clus", "node"),
        ),
        check_vma=False,
    )
```

time: 433 us -> 105 us (0.24)
  waiting for transfers between devices: 233 us -> 0 us
  Pallas kernels: 0 us -> 97.6 us
  matrix products: 58.3 us -> 0 us
  blocking collectives: 46.1 us -> 0 us
  local copies, waits for them, and re-layouts: 48.1 us -> 5.73 us
  other arithmetic: 21.1 us -> 0 us
  between operations: 14.2 us -> 0.64 us
  starting transfers between devices: 7.55 us -> 0 us
    reduce_scatter x2 -> x0, waiting for transfers between devices: 195 us -> none  [the longest x1 117 us: body(): lax.psum_scatter(grad_terms, 'node', scatter_dimension=2, tiled=True)]
    pallas_call x0 -> x1, Pallas kernels: none -> 97.6 us  [body(): pl.pallas_call(functools.partial(kernel, clusters), out_shape=(jax.ShapeD...]
    dot_general x47 -> x0, matrix products: 58.3 us -> none  [the longest x4 10.1 us: one_block(): jnp.einsum('hij,ihd->jhd', dscore, query_block, preferred_element_type=jn...]
    psum x1 -> x0, blocking collectives: 26.9 us -> none  [body(): grad_weight = lax.psum(totals[3], 'clus')]
    unnamed x4 -> x0, waiting for transfers between devices: 23.6 us -> none
    all_to_all x1 -> x0, blocking collectives: 19.2 us -> none  [body(): lax.all_to_all(jnp.stack([output_heads, query_grad_heads, key_grad_heads,...]
    all_to_all x1 -> x0, waiting for transfers between devices: 14.3 us -> none  [body(): lax.all_to_all(jnp.stack([query, keys_local, values_local, d_att]), 'node...]
    unnamed x28 -> x4, local copies, waits for them, and re-layouts: 18.8 us -> 5.73 us
  transfers between devices with their start and end apart: 4 -> 0, of which waited for: 4 -> 0; matrix products, arithmetic and copies ran while one was open for 2% -> 0% of each run, Pallas kernels for 0% -> 0%
where the time goes in v1:
time: 105 us; the launch traced here: 104 us
  Pallas kernels  97.6 us (93%)
  local copies, waits for them, and re-layouts  5.73 us (5%)
    pallas_call x1, Pallas kernels, body(): pl.pallas_call(functools.partial(kernel, clusters), out_shape=(jax.ShapeD...  97.6 us
    unnamed x4, local copies, waits for them, and re-layouts  5.73 us

profile of v1, /device:TPU:6, one launch (start us, length us, event | category | flops | bytes accessed | tf_op | source)
XLA Modules:
  0.0 104.0 jit_solution(16405919315301005751)
XLA Ops:
  0.6 97.6 %shard_map.120 = (bf16[128,1024]{1,0:T(8,128)(2,1)}, f32[64,128]{1,0:T(8,128)}, f32[1,64]{1,0:T(1,128)}, f32[4,64,64]{2,1,0:T(8,128)}) custom-call(bf16[128,1024]{1,0:T(8,128)(2,1)} %bitcast.8, bf16[128,1024]{1,0:T(8,128)(2,1)} %bitcast.9, bf16[1024,1024]{1,0:T(8,128)(2,1)} %wq_hbm.1, bf16[1024,1024]{1,0:T(8,128)(2,1)} %wk_hbm.1, bf16[1024,1024]{1,0:T(8,128)(2,1)} %wv_hbm.1, ...), custom_call_target="tpu_custom_call" | custom-call | flops 8000000000 | bytes 10000000 | tf_op jit(solution)/shard_map/pallas_call | solution.py:374
  98.2 1.7 %copy.17 = bf16[1,128,1024]{2,1,0:T(8,128)(2,1)} copy(bf16[1,128,1024]{2,1,0:T(8,128)(2,1)} %bitcast.6) | data formatting | bytes 524288
  99.9 1.4 %copy.18 = f32[1,64,128]{2,1,0:T(8,128)} copy(f32[1,64,128]{2,1,0:T(8,128)} %bitcast.7) | data formatting | bytes 65536
  101.3 1.1 %copy.19 = f32[1,64]{1,0:T(1,128)} copy(f32[1,64]{1,0:T(1,128)} %get-tuple-element.18) | data formatting | bytes 512
  102.4 1.6 %copy.20 = f32[4,64,64]{2,1,0:T(8,128)} copy(f32[4,64,64]{2,1,0:T(8,128)} %get-tuple-element.19) | data formatting | bytes 131072

commit v2 on v1

--- a/solution.py
+++ b/solution.py
@@ -30,9 +30,10 @@
     clusters,
     x_hbm, cot_hbm, wq_hbm, wk_hbm, wv_hbm, wo_hbm, eig_ref, lam_ref, mask_ref,
     gn_ref, ge_ref, gw_ref, gp_ref,
-    w, xg, cg, send, recv, eigt, qe, d0, ke, bm, eqt, dt, kt, bt,
-    acc_k, acc_v, grads, left, back, gs, gr,
-    in_sem, w_sem, ring_send, ring_recv, f_send, f_recv, b_send, b_recv, c_send, c_recv,
+    w, xlx, xly, cly, send, recv, eigt, qe, d0, ke, bm, eqt, dt, kt, bt,
+    acc_k, acc_v, grads, left, back, ha, hb, part, sums, gs, gr,
+    in_sem, w_sem, ring_send, ring_recv, f_send, f_recv, b_send, b_recv, e_send, e_recv, l_send, l_recv,
+    p_send, p_recv, c_send, c_recv,
 ):
     n = lax.axis_index("node")
     c = lax.axis_index("clus")
@@ -43,10 +44,13 @@
     def turn(i, by):
         return lax.rem(i + by, SIDE)
 
-    x_in = pltpu.make_async_copy(x_hbm, xg.at[mx, my], in_sem.at[0])
-    c_in = pltpu.make_async_copy(cot_hbm, cg.at[mx, my], in_sem.at[1])
-    x_in.start()
-    c_in.start()
+    loads = [
+        pltpu.make_async_copy(x_hbm, xlx.at[mx], in_sem.at[0]),
+        pltpu.make_async_copy(x_hbm, xly.at[my], in_sem.at[1]),
+        pltpu.make_async_copy(cot_hbm, cly.at[my], in_sem.at[2]),
+    ]
+    for load in loads:
+        load.start()
     w_hbm = (wq_hbm, wk_hbm, wv_hbm, wo_hbm)
 
     def w_copy(t, k):
@@ -78,13 +82,13 @@
     bias = jnp.where(mask_ref[...] > 0, 0.0, ABSENT)
     for j in range(NODES):
         kt[128:144, j * TOK : (j + 1) * TOK] = jnp.broadcast_to(bias[:, j : j + 1], (16, TOK)).astype(BF16)
-        part = eig_ref[:, j * TOK : (j + 1) * TOK].astype(F32)
-        full = jnp.concatenate([jnp.zeros((64, TOK), F32), part], axis=0)
+        eig_part = eig_ref[:, j * TOK : (j + 1) * TOK].astype(F32)
+        full = jnp.concatenate([jnp.zeros((64, TOK), F32), eig_part], axis=0)
         eigt[j * TOK : (j + 1) * TOK, :] = full.T.astype(BF16)
     eqt[64:128, :] = eig_ref[...]
 
-    x_in.wait()
-    c_in.wait()
+    for load in loads:
+        load.wait()
     pl.semaphore_wait(barrier, NODES - 1 + clusters - 1)
 
     def copy_to(src, dst, send_sem, recv_sem, node):
@@ -93,54 +97,33 @@
             device_id={"node": node}, device_id_type=MESH,
         )
 
-    def x_line(i, lo, size):
-        return xg.at[mx, i, pl.ds(lo, size)]
-
-    def c_line(i, lo, size):
-        return cg.at[i, my, pl.ds(lo, size)]
-
-    def x_group(i, half):
-        return xg.at[i, pl.ds(2 * half, 2)]
-
-    def c_group(i, half):
-        return cg.at[pl.ds(2 * half, 2), i]
-
-    def x_along(by):
-        return mx * SIDE + turn(my, by)
-
-    def c_along(by):
-        return turn(mx, by) * SIDE + my
+    def along_x(x):
+        return x * SIDE + my
+
+    def along_y(y):
+        return mx * SIDE + y
 
     rings = []
-    for which, line, group, one, two, p1, p2 in (
-        (0, x_line, x_group, x_along, c_along, my, mx),
-        (1, c_line, c_group, c_along, x_along, mx, my),
-    ):
+    for buf, at, to in ((xlx, mx, along_x), (xly, my, along_y), (cly, my, along_y)):
+        before, after, far = turn(at, 3), turn(at, 1), turn(at, 2)
         rings.append((
-            [(0, line(p1, 0, TOK), line(turn(p1, 3), 0, TOK), one(1)),
-             (1, line(p1, 0, TOK), line(turn(p1, 1), 0, TOK), one(3))],
-            [(2, line(turn(p1, 3), 0, 64), line(turn(p1, 2), 0, 64), one(1)),
-             (3, line(turn(p1, 1), 64, 64), line(turn(p1, 2), 64, 64), one(3))],
-            [(4, group(p2, 0), group(turn(p2, 3), 0), two(1)),
-             (5, group(p2, 1), group(turn(p2, 1), 1), two(3))],
-            [(6, group(p2, 1), group(turn(p2, 3), 1), two(1)),
-             (7, group(p2, 0), group(turn(p2, 1), 0), two(3))],
-            [(8, group(turn(p2, 3), 0), group(turn(p2, 2), 0), two(1)),
-             (9, group(turn(p2, 1), 1), group(turn(p2, 2), 1), two(3))],
+            ((0, buf.at[at], buf.at[before], to(after)), (1, buf.at[at], buf.at[after], to(before))),
+            ((2, buf.at[before, pl.ds(0, 64)], buf.at[far, pl.ds(0, 64)], to(after)),
+             (3, buf.at[after, pl.ds(64, 64)], buf.at[far, pl.ds(64, 64)], to(before))),
         ))
 
-    def ring(stage, action):
-        for which in range(2):
-            for number, out, into, node in rings[which][stage]:
-                sems = ring_send.at[which, number], ring_recv.at[which, number]
-                if action == "start":
-                    copy_to(out, out, *sems, node).start()
-                elif action == "recv":
-                    copy_to(into, into, *sems, node).wait_recv()
-                else:
-                    copy_to(out, out, *sems, node).wait_send()
-
-    ring(0, "start")
+    def ring(which, stage, action):
+        for number, out, into, node in rings[which][stage]:
+            sems = ring_send.at[which, number], ring_recv.at[which, number]
+            if action == "start":
+                copy_to(out, out, *sems, node).start()
+            elif action == "recv":
+                copy_to(into, into, *sems, node).wait_recv()
+            else:
+                copy_to(out, out, *sems, node).wait_send()
+
+    ring(0, 0, "start")
+    ring(1, 0, "start")
 
     low = lax.broadcasted_iota(jnp.int32, (TOK, 128), 1) < 64
 
@@ -153,15 +136,14 @@
     for k in range(SIDE):
         first = turn(mx, k) * SIDE
         cols = pl.ds(pl.multiple_of(first * HS, 256), 256)
-        rows_x = xg[mx, my]
+        rows_x = xly[my]
         parts = []
         for t in range(4):
             w_copy(t, k).wait()
-            rows_in = rows_x if t < 3 else cg[mx, my]
-            part = dot(rows_in, w[t, :, cols])
-            parts.append(part * SCALE if t == 0 else part)
+            product = dot(rows_x if t < 3 else cly[my], w[t, :, cols])
+            parts.append(product * SCALE if t == 0 else product)
         for pair in range(2):
-            q, kk, v, d = (part[:, pair * 128 : (pair + 1) * 128] for part in parts)
+            q, kk, v, d = (a[:, pair * 128 : (pair + 1) * 128] for a in parts)
             qs, ks, vs, ds = (pltpu.roll(a, 64, 1) for a in (q, kk, v, d))
             t0 = first + 2 * pair
             send[t0, :, 0:128] = jnp.where(low, q, ds).astype(BF16)
@@ -178,9 +160,6 @@
             @pl.when(t == n)
             def _():
                 forward_self().start()
-
-    ring(0, "recv")
-    ring(1, "start")
 
     acc_k[...] = jnp.zeros_like(acc_k)
     acc_v[...] = jnp.zeros_like(acc_v)
@@ -212,9 +191,57 @@
         kt[0:64, rows] = b_t[0:64]
         bt[:, rows] = b_t
 
-    ring(1, "recv")
-    ring(2, "start")
-    ring(3, "start")
+    ring(0, 0, "recv")
+    ring(1, 0, "recv")
+    ring(2, 0, "start")
+    ring(0, 1, "start")
+    ring(1, 1, "start")
+
+    def early(t, which):
+        tx, ty = lax.div(t, SIDE), lax.rem(t, SIDE)
+        if which == 0:
+            return grads.at[tx, ty, 1], ha.at[tx, 0, my], along_y(ty)
+        return grads.at[tx, ty, 4], hb.at[ty, 1, mx], along_x(tx)
+
+    def early_start(t):
+        for which in range(2):
+            src, dst, node = early(t, which)
+
+            @pl.when(node != n)
+            def _():
+                slot = lax.div(t, SIDE) * SIDE + my if which == 0 else lax.rem(t, SIDE) * SIDE + mx
+                copy_to(src, dst, e_send.at[which, t], e_recv.at[which, slot], node).start()
+
+            @pl.when(node == n)
+            def _():
+                slot = lax.div(t, SIDE) * SIDE + my if which == 0 else lax.rem(t, SIDE) * SIDE + mx
+                pltpu.make_async_copy(src, dst, e_recv.at[which, slot]).start()
+
+    def early_recv(which):
+        @pl.loop(0, NODES)
+        def _(slot):
+            group, head = lax.div(slot, SIDE), lax.rem(slot, SIDE)
+            own = my if which == 0 else mx
+            node = along_y(head) if which == 0 else along_x(head)
+            dst = ha.at[group, 0, head] if which == 0 else hb.at[group, 1, head]
+
+            @pl.when(head != own)
+            def _():
+                copy_to(dst, dst, e_send.at[which, slot], e_recv.at[which, slot], node).wait_recv()
+
+            @pl.when(head == own)
+            def _():
+                src = grads.at[group, my, 1] if which == 0 else grads.at[mx, group, 4]
+                pltpu.make_async_copy(src, dst, e_recv.at[which, slot]).wait()
+
+    def early_sent(which):
+        @pl.loop(0, NODES)
+        def _(t):
+            src, dst, node = early(t, which)
+
+            @pl.when(node != n)
+            def _():
+                copy_to(src, src, e_send.at[which, t], e_recv.at[which, t], node).wait_send()
 
     lane = lax.broadcasted_iota(jnp.int32, (ROWS, 128), 1)
     sub = lax.div(lax.broadcasted_iota(jnp.int32, (ROWS, 128), 0), TOK)
@@ -224,8 +251,8 @@
     def _(i):
         @pl.when(i == steps // 2)
         def _():
-            ring(2, "recv")
-            ring(4, "start")
+            ring(2, 0, "recv")
+            ring(2, 1, "start")
 
         rows = pl.ds(pl.multiple_of(i * ROWS, ROWS), ROWS)
         tile = jnp.where(lane == sub + i * (ROWS // TOK), 1.0, 0.0).astype(BF16)
@@ -242,29 +269,103 @@
         acc_k[...] += dot(eqt[:, rows], dscore)
         acc_v[...] += dot(dt[:, rows], half)
         grad_qt = grad_q.T
-        grads[0, :, rows] = (grad_qt[0:64] * SCALE).astype(BF16)
         left[:, rows] = grad_qt[64:128]
-        grads[4, :, rows] = out.T[64:128].astype(BF16)
-
-    grads[1] = acc_k[0:64].astype(BF16)
-    grads[2] = acc_v[...].astype(BF16)
+        out_t = out.T
+        for j in range(ROWS // TOK):
+            t = i * (ROWS // TOK) + j
+            cols = slice(j * TOK, (j + 1) * TOK)
+            tx, ty = lax.div(t, SIDE), lax.rem(t, SIDE)
+            grads[tx, ty, 1] = (grad_qt[0:64, cols] * SCALE).astype(BF16)
+            grads[tx, ty, 4] = out_t[64:128, cols].astype(BF16)
+            early_start(t)
+
+    for t in range(NODES):
+        cols = slice(t * TOK, (t + 1) * TOK)
+        tx, ty = divmod(t, SIDE)
+        grads[tx, ty, 2] = acc_k[0:64, cols].astype(BF16)
+        grads[tx, ty, 3] = acc_v[:, cols].astype(BF16)
+
+    def late(which, k, action):
+        own = my if which == 0 else mx
+        j = turn(own, k)
+        node = along_y(j) if which == 0 else along_x(j)
+        if which == 0:
+            src, dst, into = grads.at[:, j, 2], ha.at[:, 1, my], ha.at[:, 1, j]
+        else:
+            src, dst, into = grads.at[j, :, 3], hb.at[:, 0, mx], hb.at[:, 0, j]
+        if k == 0:
+            move = pltpu.make_async_copy(src, dst, l_recv.at[which, own])
+            if action == "start":
+                move.start()
+            elif action == "recv":
+                move.wait()
+        elif action == "start":
+            copy_to(src, dst, l_send.at[which, j], l_recv.at[which, own], node).start()
+        elif action == "recv":
+            copy_to(into, into, l_send.at[which, j], l_recv.at[which, j], node).wait_recv()
+        else:
+            copy_to(src, src, l_send.at[which, j], l_recv.at[which, own], node).wait_send()
+
+    def lines(kind, k, action):
+        own = my if kind < 2 else mx
+        j = turn(own, k)
+        node = along_y(j) if kind < 2 else along_x(j)
+        sems = p_send.at[kind, j]
+        if k == 0:
+            move = pltpu.make_async_copy(part.at[kind, own], sums.at[kind, own], p_recv.at[kind, own])
+            if action == "start":
+                move.start()
+            elif action == "recv":
+                move.wait()
+        elif action == "start":
+            copy_to(part.at[kind, j], sums.at[kind, own], sems, p_recv.at[kind, own], node).start()
+        elif action == "recv":
+            copy_to(sums.at[kind, j], sums.at[kind, j], sems, p_recv.at[kind, j], node).wait_recv()
+        else:
+            copy_to(part.at[kind, j], part.at[kind, j], sems, p_recv.at[kind, own], node).wait_send()
+
+    for which in range(2):
+        for k in (2, 1, 3, 0):
+            late(which, k, "start")
+
     left_all = left[...]
-    grads[3] = (lam * (left_all + acc_k[64:128])).astype(BF16)
+    eig_terms = (lam * (left_all + acc_k[64:128])).astype(BF16)
+    for t in range(NODES):
+        tx, ty = divmod(t, SIDE)
+        grads[tx, ty, 0] = eig_terms[:, t * TOK : (t + 1) * TOK]
+
+    def multiply(kind):
+        buf, index, rows_in = ((ha, 0, xlx), (ha, 1, xlx), (hb, 0, xly), (hb, 1, cly))[kind]
+        lhs = jnp.concatenate([buf[g, index].reshape(SIDE * HS, TOK) for g in range(SIDE)], axis=1)
+        product = dot(lhs, rows_in[...].reshape(SIDE * TOK, D))
+        part[kind] = product.astype(BF16).reshape(SIDE, HS, D)
+        for k in (2, 1, 3, 0):
+            lines(kind, k, "start")
+
+    for which in range(3):
+        if which == 2:
+            ring(2, 1, "recv")
+        else:
+            ring(which, 1, "recv")
+    early_recv(0)
+    multiply(0)
+    early_recv(1)
+    multiply(3)
+    for which in range(2):
+        for k in range(SIDE):
+            late(which, k, "recv")
+        multiply(1 + which)
 
     def backward(t):
         return copy_to(
-            grads.at[pl.ds(0, 4), :, pl.ds(pl.multiple_of(t * TOK, TOK), TOK)],
-            back.at[:, pl.ds(pl.multiple_of(n * HS, HS), HS), :],
-            b_send.at[t], b_recv.at[n], t,
+            grads.at[lax.div(t, SIDE), lax.rem(t, SIDE), pl.ds(0, 4)], landed(n), b_send.at[t], b_recv.at[n], t
         )
 
     def landed(s):
         return back.at[:, pl.ds(pl.multiple_of(s * HS, HS), HS), :]
 
     def backward_self():
-        return pltpu.make_async_copy(
-            grads.at[pl.ds(0, 4), :, pl.ds(pl.multiple_of(n * TOK, TOK), TOK)], landed(n), b_recv.at[n]
-        )
+        return pltpu.make_async_copy(grads.at[mx, my, pl.ds(0, 4)], landed(n), b_recv.at[n])
 
     backward_self().start()
 
@@ -282,8 +383,9 @@
         row_g == 0, weight_high, jnp.where(row_g == 1, weight_row - weight_high, 0.0)
     ).astype(BF16)
 
-    ring(3, "recv")
-    ring(4, "recv")
+    for kind in (0, 3, 1, 2):
+        for k in range(SIDE):
+            lines(kind, k, "recv")
 
     def across(t):
         return pltpu.make_async_remote_copy(
@@ -302,13 +404,17 @@
 
     for m in range(4):
         cols = slice(m * 256, (m + 1) * 256)
-        gx = dot(grads[0:3].reshape(192, NC), xg[:, :, :, cols].reshape(NC, 256))
-        gc = dot(grads[4], cg[:, :, :, cols].reshape(NC, 256))
-        g = jnp.concatenate([gx, gc], axis=0).T.astype(BF16)
+        stacked = []
+        for kind in range(4):
+            total = sums[kind, 0, :, cols].astype(F32)
+            for j in range(1, SIDE):
+                total += sums[kind, j, :, cols].astype(F32)
+            stacked.append(total)
+        g = jnp.concatenate(stacked, axis=0).T.astype(BF16)
         size = min(chunk, 256)
-        for part in range(256 // size):
-            owner, lo = divmod(m * 256 + part * size, chunk)
-            gs[owner, lo : lo + size, :] = g[part * size : (part + 1) * size]
+        for piece in range(256 // size):
+            owner, lo = divmod(m * 256 + piece * size, chunk)
+            gs[owner, lo : lo + size, :] = g[piece * size : (piece + 1) * size]
             if lo + size == chunk:
                 gs[owner, chunk : chunk + 16, :] = weight_part
 
@@ -329,11 +435,11 @@
 
     for m in range(4):
         rows = slice(m * 256, (m + 1) * 256)
-        total = dot(w[0, rows, :], back[0]) + dot(w[1, rows, :], back[1]) + dot(w[2, rows, :], back[2])
+        total = dot(w[0, rows, :], back[1]) + dot(w[1, rows, :], back[2]) + dot(w[2, rows, :], back[3])
         gn_ref[:, rows] = total.T.astype(BF16)
-    eig_total = back[3, 0:64, :].astype(F32)
+    eig_total = back[0, 0:64, :].astype(F32)
     for s in range(1, NODES):
-        eig_total += back[3, s * 64 : (s + 1) * 64, :].astype(F32)
+        eig_total += back[0, s * 64 : (s + 1) * 64, :].astype(F32)
     ge_ref[...] = eig_total
 
     across_self().wait()
@@ -351,8 +457,16 @@
         gp_ref[2 * pair + 1] = pltpu.roll(both, 64, 1)[:, 0:64]
     gw_ref[...] = (total[chunk : chunk + 1] + total[chunk + 1 : chunk + 2])[:, 0:64]
 
-    for stage in range(5):
-        ring(stage, "send")
+    for which in range(3):
+        for stage in range(2):
+            ring(which, stage, "send")
+    for which in range(2):
+        early_sent(which)
+        for k in range(1, SIDE):
+            late(which, k, "sent")
+    for kind in range(4):
+        for k in range(1, SIDE):
+            lines(kind, k, "sent")
 
     @pl.loop(1, NODES)
     def _(k):
@@ -366,25 +480,35 @@
             across(lax.rem(c + k, clusters)).wait_send()
 
 
+def outputs(*refs):
+    copies = [pltpu.make_async_copy(refs[i], refs[4 + i], refs[8].at[i]) for i in range(4)]
+    for copy in copies:
+        copy.start()
+    for copy in copies:
+        copy.wait()
+
+
 def body(clusters, node_feats, cotangent, w_query, w_key, w_value, w_out, eigvec, eig_weight, block_mask):
     chunk = D // clusters
     anywhere = pl.BlockSpec(memory_space=pl.ANY)
     vmem = pl.BlockSpec(memory_space=pltpu.VMEM)
     dma = pltpu.SemaphoreType.DMA
-    gn, ge, gw, gp = pl.pallas_call(
+    shapes = (
+        jax.ShapeDtypeStruct((TOK, D), BF16),
+        jax.ShapeDtypeStruct((EIG, TOK), F32),
+        jax.ShapeDtypeStruct((1, EIG), F32),
+        jax.ShapeDtypeStruct((4, chunk, HS), F32),
+    )
+    results = pl.pallas_call(
         functools.partial(kernel, clusters),
-        out_shape=(
-            jax.ShapeDtypeStruct((TOK, D), BF16),
-            jax.ShapeDtypeStruct((EIG, TOK), F32),
-            jax.ShapeDtypeStruct((1, EIG), F32),
-            jax.ShapeDtypeStruct((4, chunk, HS), F32),
-        ),
+        out_shape=shapes,
         in_specs=[anywhere] * 6 + [vmem] * 3,
         out_specs=(vmem,) * 4,
         scratch_shapes=[
             pltpu.VMEM((4, D, D), BF16),
-            pltpu.VMEM((SIDE, SIDE, TOK, D), BF16),
-            pltpu.VMEM((SIDE, SIDE, TOK, D), BF16),
+            pltpu.VMEM((SIDE, TOK, D), BF16),
+            pltpu.VMEM((SIDE, TOK, D), BF16),
+            pltpu.VMEM((SIDE, TOK, D), BF16),
             pltpu.VMEM((NODES, TOK, 256), BF16),
             pltpu.VMEM((NODES, TOK, 256), BF16),
             pltpu.VMEM((NC, 128), BF16),
@@ -398,19 +522,29 @@
             pltpu.VMEM((128, NC), BF16),
             pltpu.VMEM((128, NC), F32),
             pltpu.VMEM((64, NC), F32),
-            pltpu.VMEM((5, 64, NC), BF16),
+            pltpu.VMEM((SIDE, SIDE, 5, HS, TOK), BF16),
             pltpu.VMEM((64, NC), F32),
             pltpu.VMEM((4, D, TOK), BF16),
+            pltpu.VMEM((SIDE, 2, SIDE, HS, TOK), BF16),
+            pltpu.VMEM((SIDE, 2, SIDE, HS, TOK), BF16),
+            pltpu.VMEM((4, SIDE, HS, D), BF16),
+            pltpu.VMEM((4, SIDE, HS, D), BF16),
             pltpu.VMEM((clusters, chunk + 16, 256), BF16),
             pltpu.VMEM((clusters, chunk + 16, 256), BF16),
-            dma((2,)),
+            dma((3,)),
             dma((4, 4)),
-            dma((2, 10)),
-            dma((2, 10)),
+            dma((3, 4)),
+            dma((3, 4)),
             dma((NODES,)),
             dma((NODES,)),
             dma((NODES,)),
             dma((NODES,)),
+            dma((2, NODES)),
+            dma((2, NODES)),
+            dma((2, SIDE)),
+            dma((2, SIDE)),
+            dma((4, SIDE)),
+            dma((4, SIDE)),
             dma((clusters,)),
             dma((clusters,)),
         ],
@@ -422,6 +556,13 @@
         node_feats[0], cotangent[0], w_query, w_key, w_value, w_out,
         eigvec[0], eig_weight, block_mask[0, 0],
     )
+    gn, ge, gw, gp = pl.pallas_call(
+        outputs,
+        out_shape=shapes,
+        in_specs=[anywhere] * 4,
+        out_specs=(anywhere,) * 4,
+        scratch_shapes=[dma((4,))],
+    )(*results)
     return gn[None], ge[None], gw, gp
 
 

time: 105 us -> 104 us (level)
  local copies, waits for them, and re-layouts: 5.73 us -> 0 us
  Pallas kernels: 97.6 us -> 103 us
    unnamed x4 -> x0, local copies, waits for them, and re-layouts: 5.73 us -> none
    pallas_call x1 -> x2, Pallas kernels: 97.6 us -> 103 us  [the longest x1 89.2 us: body(): pl.pallas_call(functools.partial(kernel, clusters), out_shape=shapes, in_...]
where the time goes in v2:
time: 104 us
  Pallas kernels  103 us (99%)
    pallas_call x1, Pallas kernels, body(): pl.pallas_call(functools.partial(kernel, clusters), out_shape=shapes, in_...  89.2 us
    pallas_call x1, Pallas kernels, body(): pl.pallas_call(outputs, out_shape=shapes, in_specs=[anywhere] * 4, out_sp...  14.1 us

profile of v2, /device:TPU:6, one launch (start us, length us, event | category | flops | bytes accessed | tf_op | source)
XLA Modules:
  0.0 103.9 jit_solution(7796553656137052301)
XLA Ops:
  0.6 89.2 %shard_map.120 = (bf16[128,1024]{1,0:T(8,128)(2,1)}, f32[64,128]{1,0:T(8,128)}, f32[1,64]{1,0:T(1,128)}, f32[4,64,64]{2,1,0:T(8,128)}) custom-call(bf16[128,1024]{1,0:T(8,128)(2,1)} %bitcast.6, bf16[128,1024]{1,0:T(8,128)(2,1)} %bitcast.7, bf16[1024,1024]{1,0:T(8,128)(2,1)} %wq_hbm.1, bf16[1024,1024]{1,0:T(8,128)(2,1)} %wk_hbm.1, bf16[1024,1024]{1,0:T(8,128)(2,1)} %wv_hbm.1, ...), custom_call_target="tpu_custom_call" | custom-call | flops 8000000000 | bytes 10000000 | tf_op jit(solution)/shard_map/pallas_call | solution.py:502
  89.8 14.1 %shard_map.121 = (bf16[128,1024]{1,0:T(8,128)(2,1)}, f32[64,128]{1,0:T(8,128)}, f32[1,64]{1,0:T(1,128)}, f32[4,64,64]{2,1,0:T(8,128)}) custom-call(bf16[128,1024]{1,0:T(8,128)(2,1)} %get-tuple-element.12.refs_0_, f32[64,128]{1,0:T(8,128)} %get-tuple-element.13.refs_1_, f32[1,64]{1,0:T(1,128)} %get-tuple-element.14.refs_2_, ...), custom_call_target="tpu_custom_call" | custom-call | tf_op jit(solution)/shard_map/pallas_call | solution.py:559

commit v3 on v2

--- a/solution.py
+++ b/solution.py
@@ -31,9 +31,9 @@
     x_hbm, cot_hbm, wq_hbm, wk_hbm, wv_hbm, wo_hbm, eig_ref, lam_ref, mask_ref,
     gn_ref, ge_ref, gw_ref, gp_ref,
     w, xlx, xly, cly, send, recv, eigt, qe, d0, ke, bm, eqt, dt, kt, bt,
-    acc_k, acc_v, grads, left, back, ha, hb, part, sums, gs, gr,
+    acc_k, acc_v, grads, left, eigs, back, ha, hb, part, mid, sums, gs, gr,
     in_sem, w_sem, ring_send, ring_recv, f_send, f_recv, b_send, b_recv, e_send, e_recv, l_send, l_recv,
-    p_send, p_recv, c_send, c_recv,
+    p_send, p_recv, h_send, h_recv, c_send, c_recv,
 ):
     n = lax.axis_index("node")
     c = lax.axis_index("clus")
@@ -306,23 +306,58 @@
         else:
             copy_to(src, src, l_send.at[which, j], l_recv.at[which, own], node).wait_send()
 
-    def lines(kind, k, action):
+    def lines(kind, stage, action):
         own = my if kind < 2 else mx
+        to = along_y if kind < 2 else along_x
+        after, far, before = turn(own, 1), turn(own, 2), turn(own, 3)
+        for way in range(2):
+            if stage == 0:
+                src, dst = part.at[kind, far, pl.ds(32 * way, 32)], mid.at[kind, way]
+            else:
+                src, dst = part.at[kind, before if way else after], sums.at[kind, way]
+            number = 2 * stage + way
+            move = copy_to(
+                src, dst, p_send.at[kind, number], p_recv.at[kind, number], to(before if way else after)
+            )
+            if action == "start":
+                move.start()
+            elif action == "recv":
+                move.wait_recv()
+            else:
+                move.wait_send()
+
+    def pass_on(kind):
+        lines(kind, 0, "recv")
+        own = my if kind < 2 else mx
+        for way in range(2):
+            rows = pl.ds(32 * way, 32)
+            there = turn(own, 3 if way else 1)
+            part[kind, there, rows] = (part[kind, there, rows].astype(F32) + mid[kind, way].astype(F32)).astype(BF16)
+        lines(kind, 1, "start")
+
+    def onward(kind, k, action):
+        own, to = (mx, along_x) if kind < 2 else (my, along_y)
         j = turn(own, k)
-        node = along_y(j) if kind < 2 else along_x(j)
-        sems = p_send.at[kind, j]
+
+        def ends(sent, head):
+            if kind < 2:
+                return ha.at[sent, kind], back.at[kind, head]
+            return hb.at[sent, 0], back.at[kind, :, head]
+
+        src, dst = ends(j, own)
         if k == 0:
-            move = pltpu.make_async_copy(part.at[kind, own], sums.at[kind, own], p_recv.at[kind, own])
+            move = pltpu.make_async_copy(src, dst, h_recv.at[kind, own])
             if action == "start":
                 move.start()
             elif action == "recv":
                 move.wait()
         elif action == "start":
-            copy_to(part.at[kind, j], sums.at[kind, own], sems, p_recv.at[kind, own], node).start()
+            copy_to(src, dst, h_send.at[kind, j], h_recv.at[kind, own], to(j)).start()
         elif action == "recv":
-            copy_to(sums.at[kind, j], sums.at[kind, j], sems, p_recv.at[kind, j], node).wait_recv()
+            into = ends(j, j)[1]
+            copy_to(into, into, h_send.at[kind, j], h_recv.at[kind, j], to(j)).wait_recv()
         else:
-            copy_to(part.at[kind, j], part.at[kind, j], sems, p_recv.at[kind, own], node).wait_send()
+            copy_to(src, src, h_send.at[kind, j], h_recv.at[kind, own], to(j)).wait_send()
 
     for which in range(2):
         for k in (2, 1, 3, 0):
@@ -339,8 +374,7 @@
         lhs = jnp.concatenate([buf[g, index].reshape(SIDE * HS, TOK) for g in range(SIDE)], axis=1)
         product = dot(lhs, rows_in[...].reshape(SIDE * TOK, D))
         part[kind] = product.astype(BF16).reshape(SIDE, HS, D)
-        for k in (2, 1, 3, 0):
-            lines(kind, k, "start")
+        lines(kind, 0, "start")
 
     for which in range(3):
         if which == 2:
@@ -348,24 +382,28 @@
         else:
             ring(which, 1, "recv")
     early_recv(0)
+    early_recv(1)
     multiply(0)
-    early_recv(1)
     multiply(3)
+    for k in (2, 1, 3, 0):
+        onward(0, k, "start")
     for which in range(2):
         for k in range(SIDE):
             late(which, k, "recv")
-        multiply(1 + which)
+    pass_on(0)
+    multiply(1)
+    pass_on(3)
+    multiply(2)
+    for kind in (1, 2):
+        for k in (2, 1, 3, 0):
+            onward(kind, k, "start")
+        pass_on(kind)
 
     def backward(t):
-        return copy_to(
-            grads.at[lax.div(t, SIDE), lax.rem(t, SIDE), pl.ds(0, 4)], landed(n), b_send.at[t], b_recv.at[n], t
-        )
-
-    def landed(s):
-        return back.at[:, pl.ds(pl.multiple_of(s * HS, HS), HS), :]
+        return copy_to(grads.at[lax.div(t, SIDE), lax.rem(t, SIDE), 0], eigs.at[n], b_send.at[t], b_recv.at[n], t)
 
     def backward_self():
-        return pltpu.make_async_copy(grads.at[mx, my, pl.ds(0, 4)], landed(n), b_recv.at[n])
+        return pltpu.make_async_copy(grads.at[mx, my, 0], eigs.at[n], b_recv.at[n])
 
     backward_self().start()
 
@@ -374,88 +412,96 @@
         backward(lax.rem(n + k, NODES)).start()
 
     weight_col = jnp.sum(eig_ref[...].astype(F32) * left_all, axis=1, keepdims=True)
-    row_w = lax.broadcasted_iota(jnp.int32, (EIG, 256), 0)
-    col_w = lax.broadcasted_iota(jnp.int32, (EIG, 256), 1)
+    row_w = lax.broadcasted_iota(jnp.int32, (EIG, 128), 0)
+    col_w = lax.broadcasted_iota(jnp.int32, (EIG, 128), 1)
     weight_row = jnp.sum(jnp.where(row_w == col_w, weight_col, 0.0), axis=0, keepdims=True)
     weight_high = weight_row.astype(BF16).astype(F32)
-    row_g = lax.broadcasted_iota(jnp.int32, (16, 256), 0)
+    row_g = lax.broadcasted_iota(jnp.int32, (16, 128), 0)
     weight_part = jnp.where(
         row_g == 0, weight_high, jnp.where(row_g == 1, weight_row - weight_high, 0.0)
     ).astype(BF16)
 
-    for kind in (0, 3, 1, 2):
-        for k in range(SIDE):
-            lines(kind, k, "recv")
-
-    def across(t):
+    def rows_of(group):
+        return pl.ds(0, chunk + 16 * group)
+
+    def across(group, t):
         return pltpu.make_async_remote_copy(
-            src_ref=gs.at[t], dst_ref=gr.at[c], send_sem=c_send.at[t], recv_sem=c_recv.at[c],
+            src_ref=gs.at[group, t, rows_of(group)], dst_ref=gr.at[group, c, rows_of(group)],
+            send_sem=c_send.at[group, t], recv_sem=c_recv.at[group, c],
             device_id={"clus": t}, device_id_type=MESH,
         )
 
-    def across_in(s):
+    def across_in(group, s):
         return pltpu.make_async_remote_copy(
-            src_ref=gr.at[s], dst_ref=gr.at[s], send_sem=c_send.at[s], recv_sem=c_recv.at[s],
+            src_ref=gr.at[group, s, rows_of(group)], dst_ref=gr.at[group, s, rows_of(group)],
+            send_sem=c_send.at[group, s], recv_sem=c_recv.at[group, s],
             device_id={"clus": s}, device_id_type=MESH,
         )
 
-    def across_self():
-        return pltpu.make_async_copy(gs.at[c], gr.at[c], c_recv.at[c])
-
+    def across_self(group):
+        return pltpu.make_async_copy(
+            gs.at[group, c, rows_of(group)], gr.at[group, c, rows_of(group)], c_recv.at[group, c]
+        )
+
+    for group, kinds in enumerate(((0, 3), (1, 2))):
+        for kind in kinds:
+            lines(kind, 1, "recv")
+        for m in range(4):
+            cols = slice(m * 256, (m + 1) * 256)
+            stacked = []
+            for kind in kinds:
+                total = part[kind, my if kind < 2 else mx, :, cols].astype(F32)
+                stacked.append(total + sums[kind, 0, :, cols].astype(F32) + sums[kind, 1, :, cols].astype(F32))
+            g = jnp.concatenate(stacked, axis=0).T.astype(BF16)
+            size = min(chunk, 256)
+            for piece in range(256 // size):
+                owner, lo = divmod(m * 256 + piece * size, chunk)
+                gs[group, owner, lo : lo + size, :] = g[piece * size : (piece + 1) * size]
+                if lo + size == chunk and group == 1:
+                    gs[group, owner, chunk : chunk + 16, :] = weight_part
+        across_self(group).start()
+        if clusters > 1:
+            @pl.loop(1, clusters)
+            def _(k):
+                across(group, lax.rem(c + k, clusters)).start()
+
+    for kind in range(3):
+        for k in range(SIDE):
+            onward(kind, k, "recv")
     for m in range(4):
-        cols = slice(m * 256, (m + 1) * 256)
-        stacked = []
-        for kind in range(4):
-            total = sums[kind, 0, :, cols].astype(F32)
-            for j in range(1, SIDE):
-                total += sums[kind, j, :, cols].astype(F32)
-            stacked.append(total)
-        g = jnp.concatenate(stacked, axis=0).T.astype(BF16)
-        size = min(chunk, 256)
-        for piece in range(256 // size):
-            owner, lo = divmod(m * 256 + piece * size, chunk)
-            gs[owner, lo : lo + size, :] = g[piece * size : (piece + 1) * size]
-            if lo + size == chunk:
-                gs[owner, chunk : chunk + 16, :] = weight_part
-
-                @pl.when(c != owner)
-                def _():
-                    across(owner).start()
-
-                @pl.when(c == owner)
-                def _():
-                    across_self().start()
+        rows = slice(m * 256, (m + 1) * 256)
+        total = dot(w[0, rows, :], back[0].reshape(D, TOK))
+        total += dot(w[1, rows, :], back[1].reshape(D, TOK))
+        total += dot(w[2, rows, :], back[2].reshape(D, TOK))
+        gn_ref[:, rows] = total.T.astype(BF16)
 
     backward_self().wait()
 
     @pl.loop(1, NODES)
     def _(k):
         s = lax.rem(n + k, NODES)
-        copy_to(landed(s), landed(s), b_send.at[s], b_recv.at[s], s).wait_recv()
-
-    for m in range(4):
-        rows = slice(m * 256, (m + 1) * 256)
-        total = dot(w[0, rows, :], back[1]) + dot(w[1, rows, :], back[2]) + dot(w[2, rows, :], back[3])
-        gn_ref[:, rows] = total.T.astype(BF16)
-    eig_total = back[0, 0:64, :].astype(F32)
+        copy_to(eigs.at[s], eigs.at[s], b_send.at[s], b_recv.at[s], s).wait_recv()
+
+    eig_total = eigs[0].astype(F32)
     for s in range(1, NODES):
-        eig_total += back[0, s * 64 : (s + 1) * 64, :].astype(F32)
+        eig_total += eigs[s].astype(F32)
     ge_ref[...] = eig_total
 
-    across_self().wait()
-    if clusters > 1:
-        @pl.loop(1, clusters)
-        def _(k):
-            across_in(lax.rem(c + k, clusters)).wait_recv()
-
-    total = gr[0].astype(F32)
-    for s in range(1, clusters):
-        total += gr[s].astype(F32)
-    for pair in range(2):
-        both = total[0:chunk, pair * 128 : (pair + 1) * 128]
-        gp_ref[2 * pair] = both[:, 0:64]
-        gp_ref[2 * pair + 1] = pltpu.roll(both, 64, 1)[:, 0:64]
-    gw_ref[...] = (total[chunk : chunk + 1] + total[chunk + 1 : chunk + 2])[:, 0:64]
+    for group, kinds in enumerate(((0, 3), (1, 2))):
+        across_self(group).wait()
+        if clusters > 1:
+            @pl.loop(1, clusters)
+            def _(k):
+                across_in(group, lax.rem(c + k, clusters)).wait_recv()
+
+        used = slice(0, chunk + 16 * group)
+        total = gr[group, 0, used].astype(F32)
+        for s in range(1, clusters):
+            total += gr[group, s, used].astype(F32)
+        gp_ref[kinds[0]] = total[0:chunk, 0:64]
+        gp_ref[kinds[1]] = pltpu.roll(total[0:chunk], 64, 1)[:, 0:64]
+        if group == 1:
+            gw_ref[...] = (total[chunk : chunk + 1] + total[chunk + 1 : chunk + 2])[:, 0:64]
 
     for which in range(3):
         for stage in range(2):
@@ -465,8 +511,11 @@
         for k in range(1, SIDE):
             late(which, k, "sent")
     for kind in range(4):
+        for stage in range(2):
+            lines(kind, stage, "sent")
+    for kind in range(3):
         for k in range(1, SIDE):
-            lines(kind, k, "sent")
+            onward(kind, k, "sent")
 
     @pl.loop(1, NODES)
     def _(k):
@@ -477,15 +526,13 @@
     if clusters > 1:
         @pl.loop(1, clusters)
         def _(k):
-            across(lax.rem(c + k, clusters)).wait_send()
+            across(0, lax.rem(c + k, clusters)).wait_send()
+            across(1, lax.rem(c + k, clusters)).wait_send()
 
 
 def outputs(*refs):
-    copies = [pltpu.make_async_copy(refs[i], refs[4 + i], refs[8].at[i]) for i in range(4)]
-    for copy in copies:
-        copy.start()
-    for copy in copies:
-        copy.wait()
+    for i in range(4):
+        refs[4 + i][...] = refs[i][...]
 
 
 def body(clusters, node_feats, cotangent, w_query, w_key, w_value, w_out, eigvec, eig_weight, block_mask):
@@ -524,13 +571,15 @@
             pltpu.VMEM((64, NC), F32),
             pltpu.VMEM((SIDE, SIDE, 5, HS, TOK), BF16),
             pltpu.VMEM((64, NC), F32),
-            pltpu.VMEM((4, D, TOK), BF16),
+            pltpu.VMEM((NODES, EIG, TOK), BF16),
+            pltpu.VMEM((3, SIDE, SIDE, HS, TOK), BF16),
             pltpu.VMEM((SIDE, 2, SIDE, HS, TOK), BF16),
             pltpu.VMEM((SIDE, 2, SIDE, HS, TOK), BF16),
             pltpu.VMEM((4, SIDE, HS, D), BF16),
-            pltpu.VMEM((4, SIDE, HS, D), BF16),
-            pltpu.VMEM((clusters, chunk + 16, 256), BF16),
-            pltpu.VMEM((clusters, chunk + 16, 256), BF16),
+            pltpu.VMEM((4, 2, HS // 2, D), BF16),
+            pltpu.VMEM((4, 2, HS, D), BF16),
+            pltpu.VMEM((2, clusters, chunk + 16, 128), BF16),
+            pltpu.VMEM((2, clusters, chunk + 16, 128), BF16),
             dma((3,)),
             dma((4, 4)),
             dma((3, 4)),
@@ -545,8 +594,10 @@
             dma((2, SIDE)),
             dma((4, SIDE)),
             dma((4, SIDE)),
-            dma((clusters,)),
-            dma((clusters,)),
+            dma((3, SIDE)),
+            dma((3, SIDE)),
+            dma((2, clusters)),
+            dma((2, clusters)),
         ],
         compiler_params=pltpu.CompilerParams(
             collective_id=0, has_side_effects=True, vmem_limit_bytes=60 * 1024 * 1024
@@ -559,9 +610,8 @@
     gn, ge, gw, gp = pl.pallas_call(
         outputs,
         out_shape=shapes,
-        in_specs=[anywhere] * 4,
-        out_specs=(anywhere,) * 4,
-        scratch_shapes=[dma((4,))],
+        in_specs=[vmem] * 4,
+        out_specs=(vmem,) * 4,
     )(*results)
     return gn[None], ge[None], gw, gp
 

time: 104 us -> 90.7 us (0.87); the launches traced: 104 us -> 89.5 us
  Pallas kernels: 103 us -> 88.8 us
    pallas_call x1, Pallas kernels: 14.1 us -> 1.78 us  [body(): pl.pallas_call(outputs, out_shape=shapes, in_specs=[vmem] * 4, out_specs=...]
    pallas_call x1, Pallas kernels: 89.2 us -> 87.1 us  [body(): pl.pallas_call(functools.partial(kernel, clusters), out_shape=shapes, in_...]
where the time goes in v3:
time: 90.7 us; the launch traced here: 89.5 us
  Pallas kernels  88.8 us (98%)
    pallas_call x1, Pallas kernels, body(): pl.pallas_call(functools.partial(kernel, clusters), out_shape=shapes, in_...  87.1 us

profile of v3, /device:TPU:6, one launch (start us, length us, event | category | flops | bytes accessed | tf_op | source)
XLA Modules:
  0.0 89.5 jit_solution(18359874770010926927)
XLA Ops:
  0.6 87.1 %shard_map.120 = (bf16[128,1024]{1,0:T(8,128)(2,1)}, f32[64,128]{1,0:T(8,128)}, f32[1,64]{1,0:T(1,128)}, f32[4,64,64]{2,1,0:T(8,128)}) custom-call(bf16[128,1024]{1,0:T(8,128)(2,1)} %bitcast.6, bf16[128,1024]{1,0:T(8,128)(2,1)} %bitcast.7, bf16[1024,1024]{1,0:T(8,128)(2,1)} %wq_hbm.1, bf16[1024,1024]{1,0:T(8,128)(2,1)} %wk_hbm.1, bf16[1024,1024]{1,0:T(8,128)(2,1)} %wv_hbm.1, ...), custom_call_target="tpu_custom_call" | custom-call | flops 8000000000 | bytes 10000000 | tf_op jit(solution)/shard_map/pallas_call | solution.py:549
  87.7 1.8 %shard_map.121 = (bf16[128,1024]{1,0:T(8,128)(2,1)}, f32[64,128]{1,0:T(8,128)}, f32[1,64]{1,0:T(1,128)}, f32[4,64,64]{2,1,0:T(8,128)}) custom-call(bf16[128,1024]{1,0:T(8,128)(2,1)} %get-tuple-element.12.refs_0_, f32[64,128]{1,0:T(8,128)} %get-tuple-element.13.refs_1_, f32[1,64]{1,0:T(1,128)} %get-tuple-element.14.refs_2_, ...), custom_call_target="tpu_custom_call" | custom-call | tf_op jit(solution)/shard_map/pallas_call | solution.py:610

commit v4 on v3

--- a/solution.py
+++ b/solution.py
@@ -32,7 +32,7 @@
     gn_ref, ge_ref, gw_ref, gp_ref,
     w, xlx, xly, cly, send, recv, eigt, qe, d0, ke, bm, eqt, dt, kt, bt,
     acc_k, acc_v, grads, left, eigs, back, ha, hb, part, mid, sums, gs, gr,
-    in_sem, w_sem, ring_send, ring_recv, f_send, f_recv, b_send, b_recv, e_send, e_recv, l_send, l_recv,
+    in_sem, w_sem, ring_send, ring_recv, f_send, f_recv, b_send, b_recv, o_send, o_recv, q_send, q_recv, l_send, l_recv,
     p_send, p_recv, h_send, h_recv, c_send, c_recv,
 ):
     n = lax.axis_index("node")
@@ -57,9 +57,8 @@
         cols = pl.ds(pl.multiple_of(turn(mx, k) * 256, 256), 256)
         return pltpu.make_async_copy(w_hbm[t].at[:, cols], w.at[t, :, cols], w_sem.at[t, k])
 
-    for k in range(SIDE):
-        for t in range(4):
-            w_copy(t, k).start()
+    for t in range(4):
+        w_copy(t, 0).start()
 
     barrier = pltpu.get_barrier_semaphore()
 
@@ -140,6 +139,8 @@
         parts = []
         for t in range(4):
             w_copy(t, k).wait()
+            if k + 1 < SIDE:
+                w_copy(t, k + 1).start()
             product = dot(rows_x if t < 3 else cly[my], w[t, :, cols])
             parts.append(product * SCALE if t == 0 else product)
         for pair in range(2):
@@ -197,51 +198,45 @@
     ring(0, 1, "start")
     ring(1, 1, "start")
 
-    def early(t, which):
-        tx, ty = lax.div(t, SIDE), lax.rem(t, SIDE)
-        if which == 0:
-            return grads.at[tx, ty, 1], ha.at[tx, 0, my], along_y(ty)
-        return grads.at[tx, ty, 4], hb.at[ty, 1, mx], along_x(tx)
-
-    def early_start(t):
-        for which in range(2):
-            src, dst, node = early(t, which)
-
-            @pl.when(node != n)
-            def _():
-                slot = lax.div(t, SIDE) * SIDE + my if which == 0 else lax.rem(t, SIDE) * SIDE + mx
-                copy_to(src, dst, e_send.at[which, t], e_recv.at[which, slot], node).start()
-
-            @pl.when(node == n)
-            def _():
-                slot = lax.div(t, SIDE) * SIDE + my if which == 0 else lax.rem(t, SIDE) * SIDE + mx
-                pltpu.make_async_copy(src, dst, e_recv.at[which, slot]).start()
-
-    def early_recv(which):
-        @pl.loop(0, NODES)
-        def _(slot):
-            group, head = lax.div(slot, SIDE), lax.rem(slot, SIDE)
-            own = my if which == 0 else mx
-            node = along_y(head) if which == 0 else along_x(head)
-            dst = ha.at[group, 0, head] if which == 0 else hb.at[group, 1, head]
-
-            @pl.when(head != own)
-            def _():
-                copy_to(dst, dst, e_send.at[which, slot], e_recv.at[which, slot], node).wait_recv()
-
-            @pl.when(head == own)
-            def _():
-                src = grads.at[group, my, 1] if which == 0 else grads.at[mx, group, 4]
-                pltpu.make_async_copy(src, dst, e_recv.at[which, slot]).wait()
-
-    def early_sent(which):
-        @pl.loop(0, NODES)
-        def _(t):
-            src, dst, node = early(t, which)
-
-            @pl.when(node != n)
-            def _():
-                copy_to(src, src, e_send.at[which, t], e_recv.at[which, t], node).wait_send()
+    def early_output(tx):
+        src, dst = grads.at[tx, :, 4], hb.at[:, 1, mx]
+
+        @pl.when(tx != mx)
+        def _():
+            copy_to(src, dst, o_send.at[tx], o_recv.at[mx], along_x(tx)).start()
+
+        @pl.when(tx == mx)
+        def _():
+            pltpu.make_async_copy(src, dst, o_recv.at[mx]).start()
+
+    def early_output_wait(k, action):
+        j = turn(mx, k)
+        into = hb.at[:, 1, j]
+        if k == 0:
+            if action == "recv":
+                pltpu.make_async_copy(grads.at[mx, :, 4], into, o_recv.at[mx]).wait()
+        elif action == "recv":
+            copy_to(into, into, o_send.at[j], o_recv.at[j], along_x(j)).wait_recv()
+        else:
+            src = grads.at[j, :, 4]
+            copy_to(src, src, o_send.at[j], o_recv.at[mx], along_x(j)).wait_send()
+
+    def early_query(half, k, action):
+        j = turn(my, k)
+        groups = pl.ds(2 * half, 2)
+        src, dst, into = grads.at[groups, j, 1], ha.at[groups, 0, my], ha.at[groups, 0, j]
+        if k == 0:
+            move = pltpu.make_async_copy(src, dst, q_recv.at[half, my])
+            if action == "start":
+                move.start()
+            elif action == "recv":
+                move.wait()
+        elif action == "start":
+            copy_to(src, dst, q_send.at[half, j], q_recv.at[half, my], along_y(j)).start()
+        elif action == "recv":
+            copy_to(into, into, q_send.at[half, j], q_recv.at[half, j], along_y(j)).wait_recv()
+        else:
+            copy_to(src, src, q_send.at[half, j], q_recv.at[half, my], along_y(j)).wait_send()
 
     lane = lax.broadcasted_iota(jnp.int32, (ROWS, 128), 1)
     sub = lax.div(lax.broadcasted_iota(jnp.int32, (ROWS, 128), 0), TOK)
@@ -277,8 +272,18 @@
             tx, ty = lax.div(t, SIDE), lax.rem(t, SIDE)
             grads[tx, ty, 1] = (grad_qt[0:64, cols] * SCALE).astype(BF16)
             grads[tx, ty, 4] = out_t[64:128, cols].astype(BF16)
-            early_start(t)
-
+
+        @pl.when(lax.rem(i, 2) == 1)
+        def _():
+            early_output(lax.div(i, 2))
+
+        @pl.when(i == steps // 2 - 1)
+        def _():
+            for k in (2, 1, 3, 0):
+                early_query(0, k, "start")
+
+    for k in (2, 1, 3, 0):
+        early_query(1, k, "start")
     for t in range(NODES):
         cols = slice(t * TOK, (t + 1) * TOK)
         tx, ty = divmod(t, SIDE)
@@ -381,8 +386,10 @@
             ring(2, 1, "recv")
         else:
             ring(which, 1, "recv")
-    early_recv(0)
-    early_recv(1)
+    for k in range(SIDE):
+        early_query(0, k, "recv")
+        early_query(1, k, "recv")
+        early_output_wait(k, "recv")
     multiply(0)
     multiply(3)
     for k in (2, 1, 3, 0):
@@ -507,8 +514,10 @@
         for stage in range(2):
             ring(which, stage, "send")
     for which in range(2):
-        early_sent(which)
         for k in range(1, SIDE):
+            early_query(which, k, "sent")
+            if which == 0:
+                early_output_wait(k, "sent")
             late(which, k, "sent")
     for kind in range(4):
         for stage in range(2):
@@ -588,8 +597,10 @@
             dma((NODES,)),
             dma((NODES,)),
             dma((NODES,)),
-            dma((2, NODES)),
-            dma((2, NODES)),
+            dma((SIDE,)),
+            dma((SIDE,)),
+            dma((2, SIDE)),
+            dma((2, SIDE)),
             dma((2, SIDE)),
             dma((2, SIDE)),
             dma((4, SIDE)),

time: 90.7 us -> 90.3 us (level)
  the two profiles are of different devices: /device:TPU:6 before, /device:TPU:1 now
where the time goes in v4:
time: 90.3 us; the launch traced here: 90.1 us
  Pallas kernels  89.5 us (99%)
    pallas_call x1, Pallas kernels, body(): pl.pallas_call(functools.partial(kernel, clusters), out_shape=shapes, in_...  87.7 us

profile of v4, /device:TPU:1, one launch (start us, length us, event | category | flops | bytes accessed | tf_op | source)
XLA Modules:
  0.0 90.1 jit_solution(1491004536097636643)
XLA Ops:
  0.6 87.7 %shard_map.120 = (bf16[128,1024]{1,0:T(8,128)(2,1)}, f32[64,128]{1,0:T(8,128)}, f32[1,64]{1,0:T(1,128)}, f32[4,64,64]{2,1,0:T(8,128)}) custom-call(bf16[128,1024]{1,0:T(8,128)(2,1)} %bitcast.6, bf16[128,1024]{1,0:T(8,128)(2,1)} %bitcast.7, bf16[1024,1024]{1,0:T(8,128)(2,1)} %wq_hbm.1, bf16[1024,1024]{1,0:T(8,128)(2,1)} %wk_hbm.1, bf16[1024,1024]{1,0:T(8,128)(2,1)} %wv_hbm.1, ...), custom_call_target="tpu_custom_call" | custom-call | flops 8000000000 | bytes 10000000 | tf_op jit(solution)/shard_map/pallas_call | solution.py:558
  88.3 1.8 %shard_map.121 = (bf16[128,1024]{1,0:T(8,128)(2,1)}, f32[64,128]{1,0:T(8,128)}, f32[1,64]{1,0:T(1,128)}, f32[4,64,64]{2,1,0:T(8,128)}) custom-call(bf16[128,1024]{1,0:T(8,128)(2,1)} %get-tuple-element.12.refs_0_, f32[64,128]{1,0:T(8,128)} %get-tuple-element.13.refs_1_, f32[1,64]{1,0:T(1,128)} %get-tuple-element.14.refs_2_, ...), custom_call_target="tpu_custom_call" | custom-call | tf_op jit(solution)/shard_map/pallas_call | solution.py:621

commit v5 on v4

--- a/solution.py
+++ b/solution.py
@@ -31,15 +31,18 @@
     x_hbm, cot_hbm, wq_hbm, wk_hbm, wv_hbm, wo_hbm, eig_ref, lam_ref, mask_ref,
     gn_ref, ge_ref, gw_ref, gp_ref,
     w, xlx, xly, cly, send, recv, eigt, qe, d0, ke, bm, eqt, dt, kt, bt,
-    acc_k, acc_v, grads, left, eigs, back, ha, hb, part, mid, sums, gs, gr,
+    acc_k, acc_v, grads, left, eigs, back, ha, hb, part, mid, sums, gs, gx, gr,
     in_sem, w_sem, ring_send, ring_recv, f_send, f_recv, b_send, b_recv, o_send, o_recv, q_send, q_recv, l_send, l_recv,
-    p_send, p_recv, h_send, h_recv, c_send, c_recv,
+    p_send, p_recv, h_send, h_recv, x_send, x_recv, c_send, c_recv,
 ):
     n = lax.axis_index("node")
     c = lax.axis_index("clus")
     mx = lax.div(n, SIDE)
     my = lax.rem(n, SIDE)
     chunk = D // clusters
+    cores = 2 if clusters % 2 == 0 else 1
+    chips = clusters // cores
+    chip, core = lax.div(c, cores), lax.rem(c, cores)
 
     def turn(i, by):
         return lax.rem(i + by, SIDE)
@@ -244,7 +247,7 @@
 
     @pl.loop(0, steps)
     def _(i):
-        @pl.when(i == steps // 2)
+        @pl.when(i == steps - 2)
         def _():
             ring(2, 0, "recv")
             ring(2, 1, "start")
@@ -431,24 +434,52 @@
     def rows_of(group):
         return pl.ds(0, chunk + 16 * group)
 
+    def swap(group):
+        return pltpu.make_async_remote_copy(
+            src_ref=gs.at[group, :, 1 - core, rows_of(group)], dst_ref=gx.at[group, :, rows_of(group)],
+            send_sem=x_send.at[group], recv_sem=x_recv.at[group],
+            device_id={"clus": chip * cores + 1 - core}, device_id_type=MESH,
+        )
+
     def across(group, t):
         return pltpu.make_async_remote_copy(
-            src_ref=gs.at[group, t, rows_of(group)], dst_ref=gr.at[group, c, rows_of(group)],
-            send_sem=c_send.at[group, t], recv_sem=c_recv.at[group, c],
-            device_id={"clus": t}, device_id_type=MESH,
+            src_ref=gs.at[group, t, core, rows_of(group)], dst_ref=gr.at[group, chip, rows_of(group)],
+            send_sem=c_send.at[group, t], recv_sem=c_recv.at[group, chip],
+            device_id={"clus": t * cores + core}, device_id_type=MESH,
         )
 
     def across_in(group, s):
         return pltpu.make_async_remote_copy(
             src_ref=gr.at[group, s, rows_of(group)], dst_ref=gr.at[group, s, rows_of(group)],
             send_sem=c_send.at[group, s], recv_sem=c_recv.at[group, s],
-            device_id={"clus": s}, device_id_type=MESH,
+            device_id={"clus": s * cores + core}, device_id_type=MESH,
         )
 
     def across_self(group):
         return pltpu.make_async_copy(
-            gs.at[group, c, rows_of(group)], gr.at[group, c, rows_of(group)], c_recv.at[group, c]
+            gs.at[group, chip, core, rows_of(group)], gr.at[group, chip, rows_of(group)], c_recv.at[group, chip]
         )
+
+    def across_start(group):
+        if cores > 1:
+            swap(group).wait_recv()
+            for t in range(chips):
+                both = gs[group, t, core, 0:chunk].astype(F32) + gx[group, t, 0:chunk].astype(F32)
+                gs[group, t, core, 0:chunk] = both.astype(BF16)
+            if group == 1:
+                pair = gs[1, 0, core, chunk : chunk + 16].astype(F32) + gx[1, 0, chunk : chunk + 16].astype(F32)
+                weight_sum = jnp.sum(pair, axis=0, keepdims=True)
+                weight_top = weight_sum.astype(BF16).astype(F32)
+                weight_both = jnp.where(
+                    row_g == 0, weight_top, jnp.where(row_g == 1, weight_sum - weight_top, 0.0)
+                ).astype(BF16)
+                for t in range(chips):
+                    gs[1, t, core, chunk : chunk + 16] = weight_both
+        across_self(group).start()
+        if chips > 1:
+            @pl.loop(1, chips)
+            def _(k):
+                across(group, lax.rem(chip + k, chips)).start()
 
     for group, kinds in enumerate(((0, 3), (1, 2))):
         for kind in kinds:
@@ -463,14 +494,13 @@
             size = min(chunk, 256)
             for piece in range(256 // size):
                 owner, lo = divmod(m * 256 + piece * size, chunk)
-                gs[group, owner, lo : lo + size, :] = g[piece * size : (piece + 1) * size]
+                gs[group, owner // cores, owner % cores, lo : lo + size, :] = g[piece * size : (piece + 1) * size]
                 if lo + size == chunk and group == 1:
-                    gs[group, owner, chunk : chunk + 16, :] = weight_part
-        across_self(group).start()
-        if clusters > 1:
-            @pl.loop(1, clusters)
-            def _(k):
-                across(group, lax.rem(c + k, clusters)).start()
+                    gs[group, owner // cores, owner % cores, chunk : chunk + 16, :] = weight_part
+        if cores > 1:
+            swap(group).start()
+    across_start(0)
+    across_start(1)
 
     for kind in range(3):
         for k in range(SIDE):
@@ -496,14 +526,14 @@
 
     for group, kinds in enumerate(((0, 3), (1, 2))):
         across_self(group).wait()
-        if clusters > 1:
-            @pl.loop(1, clusters)
+        if chips > 1:
+            @pl.loop(1, chips)
             def _(k):
-                across_in(group, lax.rem(c + k, clusters)).wait_recv()
+                across_in(group, lax.rem(chip + k, chips)).wait_recv()
 
         used = slice(0, chunk + 16 * group)
         total = gr[group, 0, used].astype(F32)
-        for s in range(1, clusters):
+        for s in range(1, chips):
             total += gr[group, s, used].astype(F32)
         gp_ref[kinds[0]] = total[0:chunk, 0:64]
         gp_ref[kinds[1]] = pltpu.roll(total[0:chunk], 64, 1)[:, 0:64]
@@ -532,11 +562,14 @@
         forward(t).wait_send()
         backward(t).wait_send()
 
-    if clusters > 1:
-        @pl.loop(1, clusters)
+    if cores > 1:
+        swap(0).wait_send()
+        swap(1).wait_send()
+    if chips > 1:
+        @pl.loop(1, chips)
         def _(k):
-            across(0, lax.rem(c + k, clusters)).wait_send()
-            across(1, lax.rem(c + k, clusters)).wait_send()
+            across(0, lax.rem(chip + k, chips)).wait_send()
+            across(1, lax.rem(chip + k, chips)).wait_send()
 
 
 def outputs(*refs):
@@ -546,6 +579,8 @@
 
 def body(clusters, node_feats, cotangent, w_query, w_key, w_value, w_out, eigvec, eig_weight, block_mask):
     chunk = D // clusters
+    cores = 2 if clusters % 2 == 0 else 1
+    chips = clusters // cores
     anywhere = pl.BlockSpec(memory_space=pl.ANY)
     vmem = pl.BlockSpec(memory_space=pltpu.VMEM)
     dma = pltpu.SemaphoreType.DMA
@@ -587,8 +622,9 @@
             pltpu.VMEM((4, SIDE, HS, D), BF16),
             pltpu.VMEM((4, 2, HS // 2, D), BF16),
             pltpu.VMEM((4, 2, HS, D), BF16),
-            pltpu.VMEM((2, clusters, chunk + 16, 128), BF16),
-            pltpu.VMEM((2, clusters, chunk + 16, 128), BF16),
+            pltpu.VMEM((2, chips, cores, chunk + 16, 128), BF16),
+            pltpu.VMEM((2, chips, chunk + 16, 128), BF16),
+            pltpu.VMEM((2, chips, chunk + 16, 128), BF16),
             dma((3,)),
             dma((4, 4)),
             dma((3, 4)),
@@ -607,8 +643,10 @@
             dma((4, SIDE)),
             dma((3, SIDE)),
             dma((3, SIDE)),
-            dma((2, clusters)),
-            dma((2, clusters)),
+            dma((2,)),
+            dma((2,)),
+            dma((2, chips)),
+            dma((2, chips)),
         ],
         compiler_params=pltpu.CompilerParams(
             collective_id=0, has_side_effects=True, vmem_limit_bytes=60 * 1024 * 1024

time: 90.3 us -> 88.6 us (0.981)
  the two profiles are of different devices: /device:TPU:1 before, /device:TPU:6 now
where the time goes in v5:
time: 88.6 us; the launch traced here: 88.5 us
  Pallas kernels  87.8 us (99%)
    pallas_call x1, Pallas kernels, body(): pl.pallas_call(functools.partial(kernel, clusters), out_shape=shapes, in_...  86.1 us
    pallas_call x1, Pallas kernels, body(): pl.pallas_call(outputs, out_shape=shapes, in_specs=[vmem] * 4, out_specs=...  1.78 us

profile of v5, /device:TPU:6, one launch (start us, length us, event | category | flops | bytes accessed | tf_op | source)
XLA Modules:
  0.0 88.5 jit_solution(18073359545522680000)
XLA Ops:
  0.6 86.1 %shard_map.120 = (bf16[128,1024]{1,0:T(8,128)(2,1)}, f32[64,128]{1,0:T(8,128)}, f32[1,64]{1,0:T(1,128)}, f32[4,64,64]{2,1,0:T(8,128)}) custom-call(bf16[128,1024]{1,0:T(8,128)(2,1)} %bitcast.6, bf16[128,1024]{1,0:T(8,128)(2,1)} %bitcast.7, bf16[1024,1024]{1,0:T(8,128)(2,1)} %wq_hbm.1, bf16[1024,1024]{1,0:T(8,128)(2,1)} %wk_hbm.1, bf16[1024,1024]{1,0:T(8,128)(2,1)} %wv_hbm.1, ...), custom_call_target="tpu_custom_call" | custom-call | flops 8000000000 | bytes 10000000 | tf_op jit(solution)/shard_map/pallas_call | solution.py:593
  86.7 1.8 %shard_map.121 = (bf16[128,1024]{1,0:T(8,128)(2,1)}, f32[64,128]{1,0:T(8,128)}, f32[1,64]{1,0:T(1,128)}, f32[4,64,64]{2,1,0:T(8,128)}) custom-call(bf16[128,1024]{1,0:T(8,128)(2,1)} %get-tuple-element.12.refs_0_, f32[64,128]{1,0:T(8,128)} %get-tuple-element.13.refs_1_, f32[1,64]{1,0:T(1,128)} %get-tuple-element.14.refs_2_, ...), custom_call_target="tpu_custom_call" | custom-call | tf_op jit(solution)/shard_map/pallas_call | solution.py:659

commit v6 on v5

--- a/solution.py
+++ b/solution.py
@@ -19,7 +19,7 @@
 EIG = 64
 HS = 64
 SCALE = HS**-0.5
-ROWS = 256
+ROWS = 512
 
 
 def dot(a, b):
@@ -247,7 +247,7 @@
 
     @pl.loop(0, steps)
     def _(i):
-        @pl.when(i == steps - 2)
+        @pl.when(i == steps - 1)
         def _():
             ring(2, 0, "recv")
             ring(2, 1, "start")
@@ -276,9 +276,7 @@
             grads[tx, ty, 1] = (grad_qt[0:64, cols] * SCALE).astype(BF16)
             grads[tx, ty, 4] = out_t[64:128, cols].astype(BF16)
 
-        @pl.when(lax.rem(i, 2) == 1)
-        def _():
-            early_output(lax.div(i, 2))
+        early_output(i)
 
         @pl.when(i == steps // 2 - 1)
         def _():

time: 88.6 us -> 87.9 us (level)
  no operation moved by 1% of the time
where the time goes in v6:
time: 87.9 us; the launch traced here: 87.7 us
  Pallas kernels  87.1 us (99%)
    pallas_call x1, Pallas kernels, body(): pl.pallas_call(functools.partial(kernel, clusters), out_shape=shapes, in_...  85.3 us
    pallas_call x1, Pallas kernels, body(): pl.pallas_call(outputs, out_shape=shapes, in_specs=[vmem] * 4, out_specs=...  1.78 us

profile of v6, /device:TPU:6, one launch (start us, length us, event | category | flops | bytes accessed | tf_op | source)
XLA Modules:
  0.0 87.7 jit_solution(9676368426172058145)
XLA Ops:
  0.6 85.3 %shard_map.120 = (bf16[128,1024]{1,0:T(8,128)(2,1)}, f32[64,128]{1,0:T(8,128)}, f32[1,64]{1,0:T(1,128)}, f32[4,64,64]{2,1,0:T(8,128)}) custom-call(bf16[128,1024]{1,0:T(8,128)(2,1)} %bitcast.6, bf16[128,1024]{1,0:T(8,128)(2,1)} %bitcast.7, bf16[1024,1024]{1,0:T(8,128)(2,1)} %wq_hbm.1, bf16[1024,1024]{1,0:T(8,128)(2,1)} %wk_hbm.1, bf16[1024,1024]{1,0:T(8,128)(2,1)} %wv_hbm.1, ...), custom_call_target="tpu_custom_call" | custom-call | flops 8000000000 | bytes 10000000 | tf_op jit(solution)/shard_map/pallas_call | solution.py:591
  85.9 1.8 %shard_map.121 = (bf16[128,1024]{1,0:T(8,128)(2,1)}, f32[64,128]{1,0:T(8,128)}, f32[1,64]{1,0:T(1,128)}, f32[4,64,64]{2,1,0:T(8,128)}) custom-call(bf16[128,1024]{1,0:T(8,128)(2,1)} %get-tuple-element.12.refs_0_, f32[64,128]{1,0:T(8,128)} %get-tuple-element.13.refs_1_, f32[1,64]{1,0:T(1,128)} %get-tuple-element.14.refs_2_, ...), custom_call_target="tpu_custom_call" | custom-call | tf_op jit(solution)/shard_map/pallas_call | solution.py:657

commit v7 on v6

--- a/solution.py
+++ b/solution.py
@@ -20,6 +20,7 @@
 HS = 64
 SCALE = HS**-0.5
 ROWS = 512
+ORDER = (2, 1, 3, 0)
 
 
 def dot(a, b):
@@ -61,7 +62,7 @@
         return pltpu.make_async_copy(w_hbm[t].at[:, cols], w.at[t, :, cols], w_sem.at[t, k])
 
     for t in range(4):
-        w_copy(t, 0).start()
+        w_copy(t, ORDER[0]).start()
 
     barrier = pltpu.get_barrier_semaphore()
 
@@ -135,15 +136,15 @@
     def forward_self():
         return pltpu.make_async_copy(send.at[n], recv.at[n], f_recv.at[n])
 
-    for k in range(SIDE):
+    for at, k in enumerate(ORDER):
         first = turn(mx, k) * SIDE
         cols = pl.ds(pl.multiple_of(first * HS, 256), 256)
         rows_x = xly[my]
         parts = []
         for t in range(4):
             w_copy(t, k).wait()
-            if k + 1 < SIDE:
-                w_copy(t, k + 1).start()
+            if at + 1 < SIDE:
+                w_copy(t, ORDER[at + 1]).start()
             product = dot(rows_x if t < 3 else cly[my], w[t, :, cols])
             parts.append(product * SCALE if t == 0 else product)
         for pair in range(2):

time: 87.9 us -> 88.8 us (1.010)
  no operation moved by 1% of the time
where the time goes in v7:
time: 88.8 us; the launch traced here: 87.9 us
  Pallas kernels  87.3 us (98%)
    pallas_call x1, Pallas kernels, body(): pl.pallas_call(functools.partial(kernel, clusters), out_shape=shapes, in_...  85.5 us
    pallas_call x1, Pallas kernels, body(): pl.pallas_call(outputs, out_shape=shapes, in_specs=[vmem] * 4, out_specs=...  1.78 us

profile of v7, /device:TPU:6, one launch (start us, length us, event | category | flops | bytes accessed | tf_op | source)
XLA Modules:
  0.0 87.9 jit_solution(1725185858664667059)
XLA Ops:
  0.6 85.5 %shard_map.120 = (bf16[128,1024]{1,0:T(8,128)(2,1)}, f32[64,128]{1,0:T(8,128)}, f32[1,64]{1,0:T(1,128)}, f32[4,64,64]{2,1,0:T(8,128)}) custom-call(bf16[128,1024]{1,0:T(8,128)(2,1)} %bitcast.6, bf16[128,1024]{1,0:T(8,128)(2,1)} %bitcast.7, bf16[1024,1024]{1,0:T(8,128)(2,1)} %wq_hbm.1, bf16[1024,1024]{1,0:T(8,128)(2,1)} %wk_hbm.1, bf16[1024,1024]{1,0:T(8,128)(2,1)} %wv_hbm.1, ...), custom_call_target="tpu_custom_call" | custom-call | flops 8000000000 | bytes 10000000 | tf_op jit(solution)/shard_map/pallas_call | solution.py:592
  86.2 1.8 %shard_map.121 = (bf16[128,1024]{1,0:T(8,128)(2,1)}, f32[64,128]{1,0:T(8,128)}, f32[1,64]{1,0:T(1,128)}, f32[4,64,64]{2,1,0:T(8,128)}) custom-call(bf16[128,1024]{1,0:T(8,128)(2,1)} %get-tuple-element.12.refs_0_, f32[64,128]{1,0:T(8,128)} %get-tuple-element.13.refs_1_, f32[1,64]{1,0:T(1,128)} %get-tuple-element.14.refs_2_, ...), custom_call_target="tpu_custom_call" | custom-call | tf_op jit(solution)/shard_map/pallas_call | solution.py:658
